TPU v7x, 512 devices: a whole 4x4x16 slice. The times are simulated.
512 devices in a mesh: dp: 512 (over x, z, y, core).
Axes of the slice: x: 4, y: 4, z: 16, core: 2. Of those that a mesh axis runs over, the one named last changes fastest.
Arguments:
- embeddings: float32 [425984, 1024], P('dp'), as said below
- start_basis: float32 [425984, 256], P('dp'), may hold values from -6 to 6
Outputs:
- basis: float32 [425984, 256], P('dp')
Inputs may be any that keep to these rules, and one draw needn't show every extreme that they name: `embeddings`: rows and columns of the slab have differing scales; entries are independent within them, apart from a small common offset per column.
All inputs are finite; a program needn't handle non-finite values.
Results may differ from a plain program's by a relative error of at most 0.00015.
Values sent between devices are 32-bit elements; how exact they have to be, the bound alone decides.
A program may use at most 64 MiB of HBM per device.

v0:
```python
import jax
import jax.numpy as jnp
from jax import lax
from jax.sharding import PartitionSpec as P


def partner_2(value, axis, distance):
    mask = 2**distance
    pairs = [(source, source ^ mask) for source in range(lax.axis_size(axis))]
    return lax.ppermute(value, axis, pairs)


def tall_gram(image):
    return lax.dot_general(
        image,
        image,
        (((0,), (0,)), ((), ())),
        precision=lax.Precision.HIGHEST,
        preferred_element_type=jnp.float32,
    )


def local(embeddings, start_basis):
    count_dev = lax.axis_size("dp")
    partial_sketch = lax.dot_general(
        embeddings,
        start_basis,
        (((0,), (0,)), ((), ())),
        precision=lax.Precision.HIGHEST,
        preferred_element_type=jnp.float32,
    )
    sketch = lax.psum(partial_sketch, "dp")
    image = jnp.dot(
        embeddings, sketch, precision=lax.Precision.HIGHEST, preferred_element_type=jnp.float32
    )
    local_gram = tall_gram(image)
    lower = jnp.linalg.cholesky(local_gram)
    for bit in range(count_dev.bit_length() - 1):
        partner = partner_2(lower, "dp", bit)
        merged = jnp.dot(
            lower, lower.T, precision=lax.Precision.HIGHEST, preferred_element_type=jnp.float32
        ) + jnp.dot(
            partner, partner.T, precision=lax.Precision.HIGHEST, preferred_element_type=jnp.float32
        )
        lower = jnp.linalg.cholesky(merged)
    solved = lax.linalg.triangular_solve(
        lower, image, left_side=False, lower=True, transpose_a=True
    )
    total_rows = embeddings.shape[0] * count_dev
    return solved * jnp.sqrt(jnp.float32(total_rows))


def solution(mesh):
    in_specs = (P("dp", None), P("dp", None))
    out_specs = P("dp", None)
    return jax.shard_map(local, mesh=mesh, in_specs=in_specs, out_specs=out_specs, check_vma=False)
```

profile of v0, /device:TPU:1, one launch (start us, length us, event | category | flops | bytes accessed | tf_op | source)
XLA Modules:
  0.0 1120.8 jit_solution(9808412380356132172)
XLA Ops:
  6.5 2.0 copy-done
  8.5 8.1 fusion.81
  16.6 472.2 %all-reduce.3.cloned.1.call-done = f32[1024,256]{1,0:T(8,128)} async-done(((f32[1024,256]{1,0:T(8,128)}), f32[1024,256]{1,0:T(8,128)}) %all-reduce.3.cloned.1.call-update) | async-done | bytes 1048592 | tf_op jit(solution)/shard_map/psum | solution.py:32
  488.8 4.1 fusion.82
  493.7 2.4 fusion.83
  496.1 1.8 copy.3
  499.7 11.9 %cholesky.466 = f32[128,128]{1,0:T(8,128)S(1)} custom-call(f32[128,128]{1,0:T(8,128)S(1)} %cholesky.802), custom_call_target="Cholesky" | custom-call | tf_op jit(solution)/shard_map/jit(cholesky)/cholesky | solution.py:37
  511.6 10.4 custom-call.21
  525.6 11.7 %cholesky.483 = f32[128,128]{1,0:T(8,128)S(1)} custom-call(f32[128,128]{1,0:T(8,128)S(1)} %convolution_subtract_fusion.1), custom_call_target="Cholesky" | custom-call | tf_op jit(solution)/shard_map/jit(cholesky)/cholesky | solution.py:37
  540.9 2.7 collective-permute-start
  545.5 1.8 copy.6
  549.0 11.7 %cholesky.500 = f32[128,128]{1,0:T(8,128)S(1)} custom-call(f32[128,128]{1,0:T(8,128)S(1)} %cholesky.805), custom_call_target="Cholesky" | custom-call | tf_op jit(solution)/shard_map/jit(cholesky)/cholesky | solution.py:45
  561.5 9.8 custom-call.22
  574.1 11.7 %cholesky.517 = f32[128,128]{1,0:T(8,128)S(1)} custom-call(f32[128,128]{1,0:T(8,128)S(1)} %slice_subtract_fusion.8), custom_call_target="Cholesky" | custom-call | tf_op jit(solution)/shard_map/jit(cholesky)/cholesky | solution.py:45
  590.0 3.2 collective-permute-start.1
  593.6 5.8 collective-permute-done.1
  600.5 1.8 copy.9
  604.1 11.7 %cholesky.534 = f32[128,128]{1,0:T(8,128)S(1)} custom-call(f32[128,128]{1,0:T(8,128)S(1)} %cholesky.808), custom_call_target="Cholesky" | custom-call | tf_op jit(solution)/shard_map/jit(cholesky)/cholesky | solution.py:45
  616.5 9.8 custom-call.23
  629.1 11.7 %cholesky.551 = f32[128,128]{1,0:T(8,128)S(1)} custom-call(f32[128,128]{1,0:T(8,128)S(1)} %slice_subtract_fusion.7), custom_call_target="Cholesky" | custom-call | tf_op jit(solution)/shard_map/jit(cholesky)/cholesky | solution.py:45
  645.1 4.9 collective-permute-start.2
  650.4 4.7 collective-permute-done.2
  656.1 1.8 copy.12
  659.7 11.7 %cholesky.568 = f32[128,128]{1,0:T(8,128)S(1)} custom-call(f32[128,128]{1,0:T(8,128)S(1)} %cholesky.811), custom_call_target="Cholesky" | custom-call | tf_op jit(solution)/shard_map/jit(cholesky)/cholesky | solution.py:45
  672.2 9.8 custom-call.24
  684.7 11.7 %cholesky.585 = f32[128,128]{1,0:T(8,128)S(1)} custom-call(f32[128,128]{1,0:T(8,128)S(1)} %slice_subtract_fusion.6), custom_call_target="Cholesky" | custom-call | tf_op jit(solution)/shard_map/jit(cholesky)/cholesky | solution.py:45
  700.7 3.1 collective-permute-start.3
  704.3 4.0 collective-permute-done.3
  712.9 11.7 %cholesky.602 = f32[128,128]{1,0:T(8,128)S(1)} custom-call(f32[128,128]{1,0:T(8,128)S(1)} %cholesky.814), custom_call_target="Cholesky" | custom-call | tf_op jit(solution)/shard_map/jit(cholesky)/cholesky | solution.py:45
  725.4 9.8 custom-call.25
  737.9 11.7 %cholesky.619 = f32[128,128]{1,0:T(8,128)S(1)} custom-call(f32[128,128]{1,0:T(8,128)S(1)} %slice_subtract_fusion.5), custom_call_target="Cholesky" | custom-call | tf_op jit(solution)/shard_map/jit(cholesky)/cholesky | solution.py:45
  753.9 4.7 collective-permute-start.4
  759.0 10.8 collective-permute-done.4
  770.9 1.8 copy.18
  774.5 11.7 %cholesky.636 = f32[128,128]{1,0:T(8,128)S(1)} custom-call(f32[128,128]{1,0:T(8,128)S(1)} %cholesky.817), custom_call_target="Cholesky" | custom-call | tf_op jit(solution)/shard_map/jit(cholesky)/cholesky | solution.py:45
  786.9 9.8 custom-call.26
  799.5 11.7 %cholesky.653 = f32[128,128]{1,0:T(8,128)S(1)} custom-call(f32[128,128]{1,0:T(8,128)S(1)} %slice_subtract_fusion.4), custom_call_target="Cholesky" | custom-call | tf_op jit(solution)/shard_map/jit(cholesky)/cholesky | solution.py:45
  815.5 7.5 collective-permute-start.5
  823.4 22.0 %collective-permute-done.5 = f32[256,256]{1,0:T(8,128)S(1)} collective-permute-done((f32[256,256]{1,0:T(8,128)S(1)}, f32[256,256]{1,0:T(8,128)S(1)}, u32[]{:S(2)}, u32[]{:S(2)}) %collective-permute-start.5) | collective-permute-done | bytes 262176 | tf_op jit(solution)/shard_map/ppermute | solution.py:10
  846.4 1.8 copy.21
  850.0 11.7 %cholesky.670 = f32[128,128]{1,0:T(8,128)S(1)} custom-call(f32[128,128]{1,0:T(8,128)S(1)} %cholesky.820), custom_call_target="Cholesky" | custom-call | tf_op jit(solution)/shard_map/jit(cholesky)/cholesky | solution.py:45
  862.5 9.8 custom-call.27
  875.0 11.7 %cholesky.687 = f32[128,128]{1,0:T(8,128)S(1)} custom-call(f32[128,128]{1,0:T(8,128)S(1)} %slice_subtract_fusion.3), custom_call_target="Cholesky" | custom-call | tf_op jit(solution)/shard_map/jit(cholesky)/cholesky | solution.py:45
  891.0 10.6 collective-permute-start.6
  902.0 20.4 %collective-permute-done.6 = f32[256,256]{1,0:T(8,128)S(1)} collective-permute-done((f32[256,256]{1,0:T(8,128)S(1)}, f32[256,256]{1,0:T(8,128)S(1)}, u32[]{:S(2)}, u32[]{:S(2)}) %collective-permute-start.6) | collective-permute-done | bytes 262176 | tf_op jit(solution)/shard_map/ppermute | solution.py:10
  923.5 1.8 copy.24
  927.1 11.7 %cholesky.704 = f32[128,128]{1,0:T(8,128)S(1)} custom-call(f32[128,128]{1,0:T(8,128)S(1)} %cholesky.823), custom_call_target="Cholesky" | custom-call | tf_op jit(solution)/shard_map/jit(cholesky)/cholesky | solution.py:45
  939.5 9.8 custom-call.28
  952.1 11.7 %cholesky.721 = f32[128,128]{1,0:T(8,128)S(1)} custom-call(f32[128,128]{1,0:T(8,128)S(1)} %slice_subtract_fusion.2), custom_call_target="Cholesky" | custom-call | tf_op jit(solution)/shard_map/jit(cholesky)/cholesky | solution.py:45
  968.0 3.3 collective-permute-start.7
  971.7 5.6 collective-permute-done.7
  982.0 11.7 %cholesky.738 = f32[128,128]{1,0:T(8,128)S(1)} custom-call(f32[128,128]{1,0:T(8,128)S(1)} %cholesky.826), custom_call_target="Cholesky" | custom-call | tf_op jit(solution)/shard_map/jit(cholesky)/cholesky | solution.py:45
  994.4 9.8 custom-call.29
  1007.0 11.7 %cholesky.755 = f32[128,128]{1,0:T(8,128)S(1)} custom-call(f32[128,128]{1,0:T(8,128)S(1)} %slice_subtract_fusion.1), custom_call_target="Cholesky" | custom-call | tf_op jit(solution)/shard_map/jit(cholesky)/cholesky | solution.py:45
  1023.7 4.7 collective-permute-start.8
  1029.9 4.0 collective-permute-done.8
  1033.8 2.1 convolution_add_fusion
  1039.5 11.7 %cholesky.772 = f32[128,128]{1,0:T(8,128)S(1)} custom-call(f32[128,128]{1,0:T(8,128)S(1)} %cholesky.829), custom_call_target="Cholesky" | custom-call | tf_op jit(solution)/shard_map/jit(cholesky)/cholesky | solution.py:45
  1052.0 9.8 custom-call.30
  1064.6 11.7 %cholesky.789 = f32[128,128]{1,0:T(8,128)S(1)} custom-call(f32[128,128]{1,0:T(8,128)S(1)} %slice_subtract_fusion), custom_call_target="Cholesky" | custom-call | tf_op jit(solution)/shard_map/jit(cholesky)/cholesky | solution.py:45
  1081.3 7.2 while.1
  1082.2 2.9 bitcast_dynamic-update-slice_fusion.2
  1085.7 2.8 bitcast_dynamic-update-slice_fusion.2
  1088.5 20.5 %custom-call.11 = f32[2,128,128]{1,2,0:T(8,128)S(1)} custom-call(f32[2,128,128]{2,1,0:T(8,128)} %get-tuple-element.13), custom_call_target="InvertDiagBlocksLowerTriangular" | custom-call | tf_op jit(solution)/shard_map/triangular_solve | solution.py:46
  (156 shorter events, 109.4 us)
Async XLA Ops:
  6.5 2.0 copy-start
  6.5 482.2 %all-reduce.3.cloned.1.call-start = ((), (), s32[]{:S(2)}) async-start(), calls=%async_computation | async-start | bytes 2097152 | tf_op jit(solution)/shard_map/psum | solution.py:32
  492.8 0.9 copy-start.1
  499.0 0.7 copy-start.3
  540.9 3.5 collective-permute-start
  548.3 0.7 copy-start.4
  590.0 9.4 collective-permute-start.1
  603.4 0.7 copy-start.5
  645.1 10.0 collective-permute-start.2
  659.0 0.7 copy-start.6
  700.7 7.6 collective-permute-start.3
  712.2 0.7 copy-start.7
  753.9 15.9 %collective-permute-start.4 = (f32[256,256]{1,0:T(8,128)S(1)}, f32[256,256]{1,0:T(8,128)S(1)}, u32[]{:S(2)}, u32[]{:S(2)}) collective-permute-start(f32[256,256]{1,0:T(8,128)S(1)} %select_select_fusion.5), channel_id=1, source_target_pairs={{0,16},{1,17},{2,18},{3,19},{4,20},{5,21},{6,22},{7,23},{8,24},{9,... | collective-permute-start | bytes 786440 | tf_op jit(solution)/shard_map/ppermute | solution.py:10
  773.8 0.7 copy-start.8
  815.5 29.9 %collective-permute-start.5 = (f32[256,256]{1,0:T(8,128)S(1)}, f32[256,256]{1,0:T(8,128)S(1)}, u32[]{:S(2)}, u32[]{:S(2)}) collective-permute-start(f32[256,256]{1,0:T(8,128)S(1)} %select_select_fusion.4), channel_id=1, source_target_pairs={{0,32},{1,33},{2,34},{3,35},{4,36},{5,37},{6,38},{7,39},{8,40},{9,... | collective-permute-start | bytes 786440 | tf_op jit(solution)/shard_map/ppermute | solution.py:10
  849.3 0.7 copy-start.9
  891.0 31.4 %collective-permute-start.6 = (f32[256,256]{1,0:T(8,128)S(1)}, f32[256,256]{1,0:T(8,128)S(1)}, u32[]{:S(2)}, u32[]{:S(2)}) collective-permute-start(f32[256,256]{1,0:T(8,128)S(1)} %select_select_fusion.3), channel_id=1, source_target_pairs={{0,64},{1,65},{2,66},{3,67},{4,68},{5,69},{6,70},{7,71},{8,72},{9,... | collective-permute-start | bytes 786440 | tf_op jit(solution)/shard_map/ppermute | solution.py:10
  926.4 0.7 copy-start.10
  968.0 9.3 collective-permute-start.7
  981.3 0.7 copy-start.11
  1023.7 10.2 collective-permute-start.8
  1038.8 0.7 copy-start.2
Sparse Core Ops, SparseCore 0:
  16.7 471.9 all-reduce.2
where the time goes:
time: 1130 us; the launch traced here: 1120 us
  waiting for transfers between devices  550 us (49%)
  other arithmetic  396 us (35%)
  matrix products  61.5 us (5%)
  starting transfers between devices  44.7 us (4%)
  local copies, waits for them, and re-layouts  41.9 us (4%)
  between operations  26.8 us (2%)
    psum x1, waiting for transfers between devices, local(): sketch = lax.psum(partial_sketch, 'dp')  472 us
    another operation x63, other arithmetic, local(): lower = jnp.linalg.cholesky(merged)  317 us
    ppermute x9, waiting for transfers between devices, partner_2(): return lax.ppermute(value, axis, pairs)  77.5 us
    ppermute x9, starting transfers between devices, partner_2(): return lax.ppermute(value, axis, pairs)  44.7 us
    another operation x6, other arithmetic, local(): lower = jnp.linalg.cholesky(local_gram)  35.4 us
    another operation x18, matrix products, local(): lower = jnp.linalg.cholesky(merged)  25 us
  transfers between devices with their start and end apart: 10, of which 10 were waited for; matrix products, arithmetic and copies ran while one was open for 0% of the time, Pallas kernels for 0%

commit v1 on v0

v1 whole, which is shorter than its diff:
```python
import functools

import jax
import jax.numpy as jnp
from jax import lax
from jax.experimental import pallas as pl
from jax.experimental.pallas import tpu as pltpu
from jax.sharding import PartitionSpec as P

F32, BF16 = jnp.float32, jnp.bfloat16
NX, NZ, NY, NC = 4, 16, 4, 2
PLANE = NX * NY
D, K = 1024, 256
PARTS = 4
WIDE = D // PARTS
TILES = D // 128

PLANE_STEPS = sorted(
    [(dx, dy) for dx in range(NX) for dy in range(NY) if (dx, dy) != (0, 0)],
    key=lambda s: -(min(s[0], NX - s[0]) + min(s[1], NY - s[1])),
)
PLANE_CORE_STEPS = [(dx, dy, dc) for dx, dy in PLANE_STEPS for dc in range(NC)] + [(0, 0, 1)]
Z_STEPS = sorted(range(1, NZ), key=lambda d: -min(d, NZ - d))

NT = (((1,), (1,)), ((), ()))
NN = (((1,), (0,)), ((), ()))
TN = (((0,), (0,)), ((), ()))


def mm(a, b, dims):
    return lax.dot_general(a, b, dims, preferred_element_type=F32)


def split2(value):
    high = value.astype(BF16)
    return high, (value - high.astype(F32)).astype(BF16)


def split3(value):
    high = value.astype(BF16)
    rest = value - high.astype(F32)
    middle = rest.astype(BF16)
    return high, middle, (rest - middle.astype(F32)).astype(BF16)


def device(x, z, y, c):
    return ((x * NZ + z) * NY + y) * NC + c


def remote(src, dst, send, recv, target):
    return pltpu.make_async_remote_copy(
        src_ref=src,
        dst_ref=dst,
        send_sem=send,
        recv_sem=recv,
        device_id={"dp": target},
        device_id_type=pl.DeviceIdType.MESH,
    )


def gather_kernel(
    emb_hbm, start_hbm, image_hbm, gram_ref,
    emb, emb_hi, emb_lo, start, part, core_in, plane_in, tiles, z_in, sketch,
    image, gram_part, gram_in, gram_z, gram_all_,
    load_sem, core_s, core_r, xs, xr, zs, zr, ags, agr, bs, br, fs, fr, gs, gr, hs, hr, ks, kr, out_sem,
):
    me = lax.axis_index("dp")
    x, z, y, c = me // (NZ * NY * NC), (me // (NY * NC)) % NZ, (me // NC) % NY, me % NC
    p = x * NY + y
    plane = [((x + dx) % NX, (y + dy) % NY) for dx, dy in PLANE_STEPS]
    plane_core = [((x + dx) % NX, (y + dy) % NY, (c + dc) % NC) for dx, dy, dc in PLANE_CORE_STEPS]
    sibling = device(x, z, y, 1 - c)

    loads = [pltpu.make_async_copy(start_hbm, start, load_sem.at[PARTS])]
    loads += [
        pltpu.make_async_copy(emb_hbm.at[:, pl.ds(i * WIDE, WIDE)], emb.at[i], load_sem.at[i])
        for i in range(PARTS)
    ]
    for copy in loads:
        copy.start()

    barrier = pltpu.get_barrier_semaphore()
    for zs_ in Z_STEPS:
        pl.semaphore_signal(barrier, inc=1, device_id={"dp": device(x, (z + zs_) % NZ, y, c)}, device_id_type=pl.DeviceIdType.MESH)
    for qx, qy, qc in plane_core:
        pl.semaphore_signal(barrier, inc=1, device_id={"dp": device(qx, z, qy, qc)}, device_id_type=pl.DeviceIdType.MESH)

    loads[0].wait()
    start_hi, start_lo = split2(start[...].T)

    def core_copy(i):
        return remote(
            part.at[pl.ds((1 - c) * PLANE, PLANE), :, pl.ds(i * WIDE, WIDE)],
            core_in.at[:, :, pl.ds(i * WIDE, WIDE)],
            core_s.at[i], core_r.at[i], sibling,
        )

    for i in range(PARTS):
        loads[1 + i].wait()
        hi, lo = split2(emb[i])
        emb_hi[i] = hi
        emb_lo[i] = lo
        total = mm(start_hi, hi, NN) + (mm(start_hi, lo, NN) + mm(start_lo, hi, NN))
        part[:, :, i * WIDE:(i + 1) * WIDE] = total.reshape(NC * PLANE, 8, WIDE)
        if i == 0:
            pl.semaphore_wait(barrier, len(Z_STEPS) + len(plane_core))
        core_copy(i).start()
    own = pl.ds(c * PLANE, PLANE)
    for i in range(PARTS):
        core_copy(i).wait_recv()
        cols = slice(i * WIDE, (i + 1) * WIDE)
        part[own, :, cols] = part[own, :, cols] + core_in[:, :, cols]

    def plane_copy(o):
        qx, qy = plane[o]
        return remote(part.at[c * PLANE + qx * NY + qy], plane_in.at[o], xs.at[o], xr.at[o], device(qx, z, qy, c))

    for o in range(PLANE - 1):
        plane_copy(o).start()
    for o in range(PLANE - 1):
        plane_copy(o).wait_recv()
    total = part[c * PLANE + p]
    for o in range(PLANE - 1):
        total = total + plane_in[o]
    for t in range(TILES):
        tiles[t] = total[:, t * 128:(t + 1) * 128]

    owner = z % NC == c
    mine = z // NC
    slot = c * PLANE + p

    def z_copy(t):
        target = NC * t + c
        step = (target - z + NZ) % NZ
        return remote(tiles.at[t], z_in.at[step], zs.at[t], zr.at[step], device(x, target, y, c))

    for t in range(TILES):
        @pl.when(NC * t + c != z)
        def _(t=t):
            z_copy(t).start()

    def tile_of(t):
        return sketch.at[slot, :, pl.ds(pl.multiple_of(t * 128, 128), 128)]

    def z_out(step):
        return remote(tile_of(mine), tile_of(mine), ags.at[step], agr.at[mine], device(x, (z + step) % NZ, y, c))

    @pl.when(owner)
    def _():
        for step in Z_STEPS:
            remote(tiles.at[0], z_in.at[step], zs.at[0], zr.at[step], me).wait_recv()
        total = tiles[mine]
        for step in range(1, NZ):
            total = total + z_in[step]
        sketch[slot, :, pl.ds(pl.multiple_of(mine * 128, 128), 128)] = total
        for step in Z_STEPS:
            z_out(step).start()

    for t in range(TILES):
        @pl.when(NC * t + c != z)
        def _(t=t):
            remote(tile_of(t), tile_of(t), ags.at[0], agr.at[t], me).wait_recv()

    def plane_out(o):
        qx, qy = plane[o]
        return remote(sketch.at[slot], sketch.at[slot], bs.at[o], br.at[o], device(qx, z, qy, c))

    def source(o):
        dx, dy = PLANE_STEPS[o]
        return ((x - dx + NX) % NX) * NY + (y - dy + NY) % NY

    def forward(o):
        index = c * PLANE + (p if o == PLANE - 1 else source(o))
        return remote(sketch.at[index], sketch.at[index], fs.at[o], fr.at[o], sibling)

    for o in range(PLANE - 1):
        plane_out(o).start()
    forward(PLANE - 1).start()
    for o in reversed(range(PLANE - 1)):
        index = c * PLANE + source(o)
        remote(sketch.at[index], sketch.at[index], bs.at[o], br.at[o], me).wait_recv()
        forward(o).start()
    for o in range(PLANE):
        index = (1 - c) * PLANE + (p if o == PLANE - 1 else source(o))
        remote(sketch.at[index], sketch.at[index], fs.at[o], fr.at[o], me).wait_recv()

    total = None
    for i in range(PARTS):
        hi, lo = split2(sketch[:, :, i * WIDE:(i + 1) * WIDE].reshape(K, WIDE))
        term = mm(emb_hi[i], hi, NT) + (mm(emb_hi[i], lo, NT) + mm(emb_lo[i], hi, NT))
        total = term if total is None else total + term
    image[...] = total
    image_copy = pltpu.make_async_copy(image, image_hbm, out_sem)
    image_copy.start()
    turned = total.T
    ah, am, al = split3(turned)
    bh, bm, bl = split3(total)
    gram = mm(ah, bh, NN) + (mm(ah, bm, NN) + mm(am, bh, NN)) + (mm(am, bm, NN) + (mm(ah, bl, NN) + mm(al, bh, NN)))
    row = lax.broadcasted_iota(jnp.int32, (128, 128), 0)
    col = lax.broadcasted_iota(jnp.int32, (128, 128), 1)
    corner = gram[128:, 128:]
    diag = jnp.sum(jnp.where(row == col, corner, 0.0), axis=0, keepdims=True)
    gram_part[0:16, 0:8] = jnp.where(row >= col, gram[:128, :128], corner).reshape(16, 8, 128)
    gram_part[16:32, 0:8] = gram[:128, 128:].reshape(16, 8, 128)
    gram_part[:, 8:9] = jnp.broadcast_to(diag[None], (32, 1, 128))

    def gram_copy(o):
        qx, qy, qc = plane_core[o]
        return remote(gram_part.at[(qx * NY + qy) * NC + qc], gram_in.at[o], gs.at[o], gr.at[o], device(qx, z, qy, qc))

    for o in range(len(plane_core)):
        gram_copy(o).start()
    for o in range(len(plane_core)):
        gram_copy(o).wait_recv()
    block = p * NC + c
    total = gram_part[block]
    for o in range(len(plane_core)):
        total = total + gram_in[o]
    gram_z[z] = total

    def gram_z_copy(step):
        return remote(gram_z.at[z], gram_z.at[z], hs.at[step], hr.at[step], device(x, (z + step) % NZ, y, c))

    for step in Z_STEPS:
        gram_z_copy(step).start()
    for step in reversed(Z_STEPS):
        src = (z - step + NZ) % NZ
        remote(gram_z.at[src], gram_z.at[src], hs.at[step], hr.at[step], me).wait_recv()
    total = gram_z[0]
    for i in range(1, NZ):
        total = total + gram_z[i]
    gram_all_[block] = total

    def gram_out(o):
        qx, qy, qc = plane_core[o]
        return remote(gram_all_.at[block], gram_all_.at[block], ks.at[o], kr.at[o], device(qx, z, qy, qc))

    for o in range(len(plane_core)):
        gram_out(o).start()
    for o in reversed(range(len(plane_core))):
        dx, dy, dc = PLANE_CORE_STEPS[o]
        index = (((x - dx + NX) % NX) * NY + (y - dy + NY) % NY) * NC + (c + dc) % NC
        remote(gram_all_.at[index], gram_all_.at[index], ks.at[o], kr.at[o], me).wait_recv()
    gram_ref[...] = gram_all_[...]

    image_copy.wait()
    for i in range(PARTS):
        core_copy(i).wait_send()
    for o in range(PLANE - 1):
        plane_copy(o).wait_send()
        plane_out(o).wait_send()
    for t in range(TILES):
        @pl.when(NC * t + c != z)
        def _(t=t):
            z_copy(t).wait_send()

    @pl.when(owner)
    def _():
        for step in Z_STEPS:
            z_out(step).wait_send()
    for o in range(PLANE):
        forward(o).wait_send()
    for o in range(len(plane_core)):
        gram_copy(o).wait_send()
        gram_out(o).wait_send()
    for step in Z_STEPS:
        gram_z_copy(step).wait_send()


def sums(embeddings, start_basis):
    rows = embeddings.shape[0]
    dma = lambda n: pltpu.SemaphoreType.DMA((n,))
    vmem = pltpu.VMEM
    return pl.pallas_call(
        gather_kernel,
        out_shape=(
            jax.ShapeDtypeStruct((rows, K), F32),
            jax.ShapeDtypeStruct((32, 9, 128), F32),
        ),
        in_specs=[pl.BlockSpec(memory_space=pl.ANY)] * 2,
        out_specs=(pl.BlockSpec(memory_space=pl.ANY), pl.BlockSpec(memory_space=pltpu.VMEM)),
        scratch_shapes=[
            vmem((PARTS, rows, WIDE), F32),
            vmem((PARTS, rows, WIDE), BF16),
            vmem((PARTS, rows, WIDE), BF16),
            vmem((rows, K), F32),
            vmem((NC * PLANE, 8, D), F32),
            vmem((PLANE, 8, D), F32),
            vmem((PLANE - 1, 8, D), F32),
            vmem((TILES, 8, 128), F32),
            vmem((NZ, 8, 128), F32),
            vmem((NC * PLANE, 8, D), F32),
            vmem((rows, K), F32),
            vmem((32, 9, 128), F32),
            vmem((31, 9, 128), F32),
            vmem((NZ, 9, 128), F32),
            vmem((32, 9, 128), F32),
            dma(PARTS + 1),
            dma(PARTS), dma(PARTS),
            dma(PLANE), dma(PLANE),
            dma(TILES), dma(NZ),
            dma(NZ), dma(TILES),
            dma(PLANE), dma(PLANE),
            dma(PLANE), dma(PLANE),
            dma(32), dma(32),
            dma(NZ), dma(NZ),
            dma(32), dma(32),
            pltpu.SemaphoreType.DMA,
        ],
        compiler_params=pltpu.CompilerParams(
            collective_id=0, has_side_effects=True, vmem_limit_bytes=48 << 20
        ),
        name="sums",
    )(embeddings, start_basis)


def factor_block(cols, strips, size):
    rows = lax.broadcasted_iota(jnp.int32, (size, 128), 0)
    scale = jnp.zeros((size, 128), F32)
    for j in range(0, size, 2):
        cj, cn = cols[j], cols[j + 1]
        a, b, d = cj[j:j + 1], cj[j + 1:j + 2], cn[j + 1:j + 2]
        q = 1.0 / (a * d - b * b)
        aq, bq, dq = a * q, b * q, d * q
        u = cj * dq - cn * bq
        v = cn * aq - cj * bq
        for k in range(j + 2, size):
            lo = (k // 8) * 8
            new = cols[k][lo:] - (u[lo:] * cj[k:k + 1] + v[lo:] * cn[k:k + 1])
            cols[k] = jnp.concatenate([cols[k][:lo], new], 0) if lo else new
        below = rows > j + 1
        ba = b * (1.0 / a)
        um = jnp.where(below, u, jnp.where(rows == j + 1, ba, 0.0))
        vm = jnp.where(below, v, 0.0)
        strips = [s - (um * s[j:j + 1] + vm * s[j + 1:j + 2]) for s in strips]
        ra = lax.rsqrt(a)
        rd = lax.rsqrt(d - ba * b)
        scale = jnp.where(rows == j, ra, jnp.where(rows == j + 1, rd, scale))
    return [s * scale for s in strips]


def cholesky_inverse(work, size):
    n = work.shape[0]
    for k in range(n // size):
        r0 = k * size
        use = [0, 1, 2] if r0 < 128 else [1, 2, 3]
        strips = {i: work[r0:r0 + size, 128 * i:128 * (i + 1)] for i in use}
        off = r0 % 128
        base = strips[r0 // 128]
        cols = [jnp.broadcast_to(base[:, off + j:off + j + 1], (size, 128)) for j in range(size)]
        done = dict(zip(use, factor_block(cols, [strips[i] for i in use], size)))
        for i in use:
            if i >= 2:
                work[r0:r0 + size, 128 * i:128 * (i + 1)] = done[i]
        rest = r0 + size
        if rest == n:
            break
        low = (rest // 128) * 128
        pieces = {i: split3(done[i]) for i in use}
        ahead = [i for i in use if i < 2 and i * 128 >= low]
        h, m, l = [jnp.concatenate([pieces[i][t] for i in ahead], 1) for t in range(3)]
        left = jnp.concatenate([h, h, m, h, l, m], 0)
        for i in use:
            if i < 2 and (i + 1) * 128 <= rest:
                continue
            h, m, l = pieces[i]
            change = mm(left, jnp.concatenate([h, m, h, l, h, m], 0), TN)
            cols_i = slice(128 * i, 128 * (i + 1))
            work[rest:n, cols_i] = work[rest:n, cols_i] - change[rest - low:]


def basis_kernel(scale, gram_ref, image_hbm, out_ref, image, work, sem):
    copy = pltpu.make_async_copy(image_hbm, image, sem)
    copy.start()
    row = lax.broadcasted_iota(jnp.int32, (128, 128), 0)
    col = lax.broadcasted_iota(jnp.int32, (128, 128), 1)
    both = gram_ref[0:16, 0:8].reshape(128, 128)
    cross = gram_ref[16:32, 0:8].reshape(128, 128)
    last = gram_ref[0, 8:9]
    turned = both.T
    diag = row == col
    first = jnp.where(row >= col, both, turned)
    corner = jnp.where(diag, last, jnp.where(row < col, both, turned))
    row1 = lax.rsqrt(jnp.sum(jnp.where(diag, first, 0.0), axis=0, keepdims=True))
    row2 = lax.rsqrt(last)
    col1 = lax.rsqrt(jnp.sum(jnp.where(diag, first, 0.0), axis=1, keepdims=True))
    col2 = lax.rsqrt(jnp.sum(jnp.where(diag, corner, 0.0), axis=1, keepdims=True))
    eye = jnp.where(diag, 1.0, 0.0)
    zero = jnp.zeros((128, 128), F32)
    work[:128, 0:128] = first * col1 * row1
    work[:128, 128:256] = cross * col1 * row2
    work[128:, 128:256] = corner * col2 * row2
    work[:128, 256:384] = eye
    work[:128, 384:512] = zero
    work[128:, 256:384] = zero
    work[128:, 384:512] = eye
    cholesky_inverse(work, 16)
    factor = jnp.concatenate([work[:, 256:384] * (row1 * scale), work[:, 384:512] * (row2 * scale)], 1)
    fh, fl = split2(factor)
    copy.wait()
    hi, lo = split2(image[...])
    out_ref[...] = mm(hi, fh, NT) + (mm(hi, fl, NT) + mm(lo, fh, NT))


def basis_of(gram, image, scale):
    rows = image.shape[0]
    return pl.pallas_call(
        functools.partial(basis_kernel, scale),
        out_shape=jax.ShapeDtypeStruct((rows, K), F32),
        in_specs=[pl.BlockSpec(memory_space=pltpu.VMEM), pl.BlockSpec(memory_space=pl.ANY)],
        out_specs=pl.BlockSpec(memory_space=pltpu.VMEM),
        scratch_shapes=[
            pltpu.VMEM((rows, K), F32),
            pltpu.VMEM((K, 2 * K), F32),
            pltpu.SemaphoreType.DMA,
        ],
        compiler_params=pltpu.CompilerParams(vmem_limit_bytes=48 << 20),
        name="basis",
    )(gram, image)


def local(embeddings, start_basis):
    total_rows = embeddings.shape[0] * lax.axis_size("dp")
    image, gram = sums(embeddings, start_basis)
    return basis_of(gram, image, float(total_rows) ** 0.5)


def solution(mesh):
    in_specs = (P("dp", None), P("dp", None))
    out_specs = P("dp", None)
    return jax.shard_map(local, mesh=mesh, in_specs=in_specs, out_specs=out_specs, check_vma=False)
```

time: 1130 us -> 89.1 us (0.08)
  waiting for transfers between devices: 550 us -> 0 us
  other arithmetic: 396 us -> 0 us
  Pallas kernels: 0 us -> 85.6 us
  matrix products: 61.5 us -> 0 us
  starting transfers between devices: 44.7 us -> 0 us
  local copies, waits for them, and re-layouts: 41.9 us -> 3.12 us
  between operations: 26.8 us -> 0.17 us
    psum x1 -> x0, waiting for transfers between devices: 472 us -> none  [local(): sketch = lax.psum(partial_sketch, 'dp')]
    another operation x72 -> x0, other arithmetic: 375 us -> none  [the longest x63 317 us: local(): lower = jnp.linalg.cholesky(merged)]
    pallas_call x0 -> x2, Pallas kernels: none -> 85.6 us  [the longest x1 76.8 us: sums(): pl.pallas_call(gather_kernel, out_shape=(jax.ShapeDtypeStruct((rows, K),...]
    ppermute x9 -> x0, waiting for transfers between devices: 77.5 us -> none  [partner_2(): return lax.ppermute(value, axis, pairs)]
    ppermute x9 -> x0, starting transfers between devices: 44.7 us -> none  [partner_2(): return lax.ppermute(value, axis, pairs)]
    another operation x23 -> x0, matrix products: 31.3 us -> none  [the longest x18 25 us: local(): lower = jnp.linalg.cholesky(merged)]
    dot_general x21 -> x0, matrix products: 30.3 us -> none  [the longest x9 11 us: local(): jnp.dot(partner, partner.T, precision=lax.Precision.HIGHEST, preferred_el...]
    add x9 -> x0, local copies, waits for them, and re-layouts: 16 us -> none  [local(): jnp.dot(lower, lower.T, precision=lax.Precision.HIGHEST, preferred_elemen...]
  transfers between devices with their start and end apart: 10 -> 0, of which waited for: 10 -> 0; matrix products, arithmetic and copies ran while one was open for 0% -> 0% of each run, Pallas kernels for 0% -> 0%
where the time goes in v1:
time: 89.1 us; the launch traced here: 88.9 us
  Pallas kernels  85.6 us (96%)
  local copies, waits for them, and re-layouts  3.12 us (4%)
    pallas_call x1, Pallas kernels, sums(): pl.pallas_call(gather_kernel, out_shape=(jax.ShapeDtypeStruct((rows, K),...  76.8 us
    pallas_call x1, Pallas kernels, basis_of(): pl.pallas_call(functools.partial(basis_kernel, scale), out_shape=jax.Shap...  8.87 us
    unnamed x4, local copies, waits for them, and re-layouts  3.12 us

profile of v1, /device:TPU:1, one launch (start us, length us, event | category | flops | bytes accessed | tf_op | source)
XLA Modules:
  0.0 88.9 jit_solution(3472472748289023417)
XLA Ops:
  0.0 0.0 copy-start
  0.0 2.0 %copy-done = f32[832,1024]{1,0:T(8,128)S(1)} copy-done((f32[832,1024]{1,0:T(8,128)S(1)}, f32[832,1024]{1,0:T(8,128)}, u32[]{:S(2)}) %copy-start) | copy-done | bytes 3407896
  2.0 0.0 copy-start.1
  2.0 1.2 %copy-done.1 = f32[832,256]{1,0:T(8,128)S(1)} copy-done((f32[832,256]{1,0:T(8,128)S(1)}, f32[832,256]{1,0:T(8,128)}, u32[]{:S(2)}) %copy-start.1) | copy-done | bytes 851992
  3.1 76.8 %sums.1 = (f32[832,256]{1,0:T(8,128)S(1)}, f32[32,9,128]{2,1,0:T(8,128)S(1)}) custom-call(f32[832,1024]{1,0:T(8,128)S(1)} %copy-done, f32[832,256]{1,0:T(8,128)S(1)} %copy-done.1), custom_call_target="tpu_custom_call" | custom-call | tf_op jit(solution)/shard_map/sums/pallas_call | solution.py:274
  79.9 8.9 %basis.1 = f32[832,256]{1,0:T(8,128)} custom-call(f32[32,9,128]{2,1,0:T(8,128)S(1)} %get-tuple-element.7.gram_ref, f32[832,256]{1,0:T(8,128)S(1)} %get-tuple-element.8.image_hbm), custom_call_target="tpu_custom_call" | custom-call | tf_op jit(solution)/shard_map/basis/pallas_call | solution.py:407
Async XLA Ops:
  0.0 2.0 %copy-start = (f32[832,1024]{1,0:T(8,128)S(1)}, f32[832,1024]{1,0:T(8,128)}, u32[]{:S(2)}) copy-start(f32[832,1024]{1,0:T(8,128)} %emb_hbm.1) | copy-start | bytes 10223620
  2.0 1.2 %copy-start.1 = (f32[832,256]{1,0:T(8,128)S(1)}, f32[832,256]{1,0:T(8,128)}, u32[]{:S(2)}) copy-start(f32[832,256]{1,0:T(8,128)} %start_hbm.1) | copy-start | bytes 2555908

commit v2 on v0

v2 whole, which is shorter than its diff:
```python
import functools

import jax
import jax.numpy as jnp
from jax import lax
from jax.experimental import pallas as pl
from jax.experimental.pallas import tpu as pltpu
from jax.sharding import PartitionSpec as P

F32, BF16 = jnp.float32, jnp.bfloat16
NX, NZ, NY, NC = 4, 16, 4, 2
PLANE = NX * NY
D, K = 1024, 256
PARTS = 4
WIDE = D // PARTS
HALVES = 2
HALF = K // HALVES
OWN = D // NC
OWN_TILES = OWN // 128
BLOCK = 16
VMEM_BYTES = 60 << 20

PLANE_STEPS = sorted(
    [(dx, dy) for dx in range(NX) for dy in range(NY) if (dx, dy) != (0, 0)],
    key=lambda s: -(min(s[0], NX - s[0]) + min(s[1], NY - s[1])),
)
PLANE_CORE_STEPS = [(dx, dy, dc) for dx, dy in PLANE_STEPS for dc in range(NC)] + [(0, 0, 1)]
Z_STEPS = sorted(range(1, NZ), key=lambda d: -min(d, NZ - d))

NT = (((1,), (1,)), ((), ()))
NN = (((1,), (0,)), ((), ()))
TN = (((0,), (0,)), ((), ()))


def mm(a, b, dims):
    return lax.dot_general(a, b, dims, preferred_element_type=F32)


def split2(value):
    high = value.astype(BF16)
    return high, (value - high.astype(F32)).astype(BF16)


def split3(value):
    high = value.astype(BF16)
    rest = value - high.astype(F32)
    middle = rest.astype(BF16)
    return high, middle, (rest - middle.astype(F32)).astype(BF16)


def device(x, z, y, c):
    return ((x * NZ + z) * NY + y) * NC + c


def remote(src, dst, send, recv, target):
    return pltpu.make_async_remote_copy(
        src_ref=src,
        dst_ref=dst,
        send_sem=send,
        recv_sem=recv,
        device_id={"dp": target},
        device_id_type=pl.DeviceIdType.MESH,
    )


def offset(x, y, dx, dy):
    return ((x + dx) % NX) * NY + (y + dy) % NY


def gather_kernel(
    emb_hbm, start_hbm, image_hbm, gram_ref, first_ref,
    emb, emb_hi, emb_lo, start, give, core_in, part, plane_in, tiles, z_in, sketch,
    image, gram_part, gram_in_a, gram_in_b, gram_z_a, gram_z_b, gram_all,
    load_sem, core_s, core_r, xs, xr, zs, zr, ags, agr, bs, br, fs, fr,
    gas, gar, gbs, gbr, has, har, hbs, hbr, kas, kar, kbs, kbr, out_sem,
):
    me = lax.axis_index("dp")
    x, z, y, c = me // (NZ * NY * NC), (me // (NY * NC)) % NZ, (me // NC) % NY, me % NC
    p = x * NY + y
    sibling = device(x, z, y, 1 - c)
    around = [(0, 0)] + PLANE_STEPS

    def at(q, core):
        return device(q // NY, z, q % NY, core)

    places = [NC * (1 - c), NC * (1 - c) + 1, NC * c, NC * c + 1]

    def wide(i):
        return pl.ds(pl.multiple_of(places[i] * WIDE, WIDE), WIDE)

    loads = [pltpu.make_async_copy(start_hbm, start, load_sem.at[PARTS])]
    loads += [pltpu.make_async_copy(emb_hbm.at[:, wide(i)], emb.at[i], load_sem.at[i]) for i in range(PARTS)]
    for copy in loads:
        copy.start()

    barrier = pltpu.get_barrier_semaphore()
    greeted = [device(x, (z + step) % NZ, y, c) for step in Z_STEPS]
    greeted += [at(offset(x, y, dx, dy), (c + dc) % NC) for dx, dy, dc in PLANE_CORE_STEPS]
    for other in greeted:
        pl.semaphore_signal(barrier, inc=1, device_id={"dp": other}, device_id_type=pl.DeviceIdType.MESH)

    loads[0].wait()
    start_hi, start_lo = split2(start[...].T)

    def core_copy(i):
        return remote(give.at[i], core_in.at[i], core_s.at[i], core_r.at[i], sibling)

    for i in range(PARTS):
        loads[1 + i].wait()
        hi, lo = split2(emb[i])
        emb_hi[i] = hi
        emb_lo[i] = lo
        total = mm(start_hi, hi, NN) + (mm(start_hi, lo, NN) + mm(start_lo, hi, NN))
        total = total.reshape(HALVES, PLANE, 8, WIDE)
        if i < NC:
            give[i] = total
            if i == 0:
                pl.semaphore_wait(barrier, len(greeted))
            core_copy(i).start()
        else:
            j = i - NC
            core_copy(j).wait_recv()
            part[:, :, :, j * WIDE:(j + 1) * WIDE] = total + core_in[j]

    def plane_copy(h, o):
        q = offset(x, y, *PLANE_STEPS[o])
        return remote(part.at[h, q], plane_in.at[h, o], xs.at[h, o], xr.at[h, o], at(q, c))

    for h in range(HALVES):
        for o in range(PLANE - 1):
            plane_copy(h, o).start()

    def keeper(h, t):
        return 4 * t + NC * h + c

    def z_copy(h, t):
        step = (keeper(h, t) - z + NZ) % NZ
        return remote(tiles.at[h, t], z_in.at[step], zs.at[h, t], zr.at[step], device(x, keeper(h, t), y, c))

    for h in range(HALVES):
        for o in range(PLANE - 1):
            plane_copy(h, o).wait_recv()
        total = part[h, p]
        for o in range(PLANE - 1):
            total = total + plane_in[h, o]
        for t in range(OWN_TILES):
            tiles[h, t] = total[:, t * 128:(t + 1) * 128]
        for t in range(OWN_TILES):
            @pl.when(keeper(h, t) != z)
            def _(h=h, t=t):
                z_copy(h, t).start()

    def lanes(start, size):
        return pl.ds(pl.multiple_of(start, 128), size)

    def tile_of(h, t):
        return sketch.at[h, p, :, lanes(c * OWN + t * 128, 128)]

    mine = z // 4

    def z_out(h, step):
        return remote(tile_of(h, mine), tile_of(h, mine), ags.at[step], agr.at[h, mine], device(x, (z + step) % NZ, y, c))

    def keeps(h):
        return z % 4 == NC * h + c

    for h in range(HALVES):
        @pl.when(keeps(h))
        def _(h=h):
            for step in reversed(Z_STEPS):
                remote(tiles.at[0, 0], z_in.at[step], zs.at[0, 0], zr.at[step], me).wait_recv()
            total = tiles[h, mine]
            for step in range(1, NZ):
                total = total + z_in[step]
            sketch[h, p, :, lanes(c * OWN + mine * 128, 128)] = total
            for step in Z_STEPS:
                z_out(h, step).start()

    def block_of(h, q, core):
        return sketch.at[h, q, :, lanes(core * OWN, OWN)]

    def plane_out(h, o):
        q = offset(x, y, *PLANE_STEPS[o])
        return remote(block_of(h, p, c), block_of(h, p, c), bs.at[h, o], br.at[h, o], at(q, c))

    def source(o):
        if o == PLANE - 1:
            return p
        dx, dy = PLANE_STEPS[o]
        return offset(x, y, -dx, -dy)

    def forward(h, o):
        return remote(block_of(h, source(o), c), block_of(h, source(o), c), fs.at[h, o], fr.at[h, o], sibling)

    for h in range(HALVES):
        for t in range(OWN_TILES):
            @pl.when(keeper(h, t) != z)
            def _(h=h, t=t):
                remote(tile_of(h, t), tile_of(h, t), ags.at[0], agr.at[h, t], me).wait_recv()
        for o in range(PLANE - 1):
            plane_out(h, o).start()
        forward(h, PLANE - 1).start()

    def image_part(h, core):
        total = None
        for j in range(NC):
            i = (NC if core is c else 0) + j
            block = sketch[h, :, :, lanes(core * OWN + j * WIDE, WIDE)]
            hi, lo = split2(block.reshape(PLANE * 8, WIDE))
            term = mm(emb_hi[i], hi, NT) + (mm(emb_hi[i], lo, NT) + mm(emb_lo[i], hi, NT))
            total = term if total is None else total + term
        return total

    halves = []
    for h in range(HALVES):
        for o in reversed(range(PLANE - 1)):
            block = block_of(h, source(o), c)
            remote(block, block, bs.at[h, o], br.at[h, o], me).wait_recv()
            forward(h, o).start()
        halves.append(image_part(h, c))

    keeps_a = y % NC == c

    def gram_a(s):
        q = offset(x, y, *around[s])
        return remote(gram_part.at[0, q], gram_in_a.at[NC * s + c], gas.at[s], gar.at[NC * s + c], at(q, (q % NY) % NC))

    def gram_b(s, dc):
        q, core = offset(x, y, *around[s]), (c + dc) % NC
        return remote(gram_part.at[1 + core, q], gram_in_b.at[NC * s + c], gbs.at[NC * s + dc], gbr.at[NC * s + c], at(q, core))

    pairs = [(s, dc) for s in range(PLANE) for dc in range(NC) if (s, dc) != (0, 0)]

    turned = []
    for h in range(HALVES):
        for o in range(PLANE):
            block = block_of(h, source(o), 1 - c)
            remote(block, block, fs.at[h, o], fr.at[h, o], me).wait_recv()
        value = halves[h] + image_part(h, 1 - c)
        image[:, h * HALF:(h + 1) * HALF] = value
        turned.append(split2(value.T))
        bh, bl = split2(value)
        for g in range(h + 1):
            ah, al = turned[g]
            gram = mm(ah, bh, NN) + (mm(ah, bl, NN) + mm(al, bh, NN)) + mm(al, bl, NN)
            gram_part[h + g] = gram.reshape(PLANE, 8, 128)
        if h == 0:
            for s in range(1, PLANE):
                gram_a(s).start()

            @pl.when(jnp.logical_not(keeps_a))
            def _():
                gram_a(0).start()
        else:
            for s, dc in pairs:
                gram_b(s, dc).start()
    image_copy = pltpu.make_async_copy(image, image_hbm, out_sem)
    image_copy.start()

    def gram_z_copy(store, send, recv, step):
        return remote(store.at[z], store.at[z], send.at[step], recv.at[step], device(x, (z + step) % NZ, y, c))

    @pl.when(keeps_a)
    def _():
        total = gram_part[0, p]
        for s, dc in pairs:
            slot = NC * s + (c + dc) % NC
            remote(gram_part.at[0, 0], gram_in_a.at[slot], gas.at[0], gar.at[slot], me).wait_recv()
            total = total + gram_in_a[slot]
        gram_z_a[z] = total
        for step in Z_STEPS:
            gram_z_copy(gram_z_a, has, har, step).start()

    total = gram_part[1 + c, p]
    for s, dc in pairs:
        slot = NC * s + (c + dc) % NC
        remote(gram_part.at[0, 0], gram_in_b.at[slot], gbs.at[0], gbr.at[slot], me).wait_recv()
        total = total + gram_in_b[slot]
    gram_z_b[z] = total
    for step in Z_STEPS:
        gram_z_copy(gram_z_b, hbs, hbr, step).start()

    def z_sum(store, send, recv):
        for step in reversed(Z_STEPS):
            src = (z - step + NZ) % NZ
            remote(store.at[src], store.at[src], send.at[step], recv.at[step], me).wait_recv()
        total = store[0]
        for i in range(1, NZ):
            total = total + store[i]
        return total

    def gram_out_a(s, dc):
        block = gram_all.at[0, p]
        return remote(block, block, kas.at[NC * s + dc], kar.at[p], at(offset(x, y, *around[s]), (c + dc) % NC))

    def gram_out_b(s, dc):
        block = gram_all.at[1 + c, p]
        return remote(block, block, kbs.at[NC * s + dc], kbr.at[c, p], at(offset(x, y, *around[s]), (c + dc) % NC))

    @pl.when(keeps_a)
    def _():
        gram_all[0, p] = z_sum(gram_z_a, has, har)
        for s, dc in pairs:
            gram_out_a(s, dc).start()

    gram_all[1 + c, p] = z_sum(gram_z_b, hbs, hbr)
    for s, dc in pairs:
        gram_out_b(s, dc).start()

    for s in range(1, PLANE):
        q = offset(x, y, *around[s])
        remote(gram_all.at[0, q], gram_all.at[0, q], kas.at[0], kar.at[q], me).wait_recv()

    @pl.when(jnp.logical_not(keeps_a))
    def _():
        remote(gram_all.at[0, p], gram_all.at[0, p], kas.at[0], kar.at[p], me).wait_recv()

    first_ref[...] = first_inverse(gram_all[0].reshape(HALF, HALF))

    for s, dc in pairs:
        q, core = offset(x, y, *around[s]), (c + dc) % NC
        remote(gram_all.at[1 + core, q], gram_all.at[1 + core, q], kbs.at[0], kbr.at[core, q], me).wait_recv()
    gram_ref[...] = gram_all[1:3].reshape(NC, HALF, HALF)

    image_copy.wait()
    for i in range(NC):
        core_copy(i).wait_send()
    for h in range(HALVES):
        for o in range(PLANE - 1):
            plane_copy(h, o).wait_send()
            plane_out(h, o).wait_send()
        for o in range(PLANE):
            forward(h, o).wait_send()
        for t in range(OWN_TILES):
            @pl.when(keeper(h, t) != z)
            def _(h=h, t=t):
                z_copy(h, t).wait_send()

        @pl.when(keeps(h))
        def _(h=h):
            for step in Z_STEPS:
                z_out(h, step).wait_send()
    for s in range(1, PLANE):
        gram_a(s).wait_send()

    @pl.when(jnp.logical_not(keeps_a))
    def _():
        gram_a(0).wait_send()

    @pl.when(keeps_a)
    def _():
        for step in Z_STEPS:
            gram_z_copy(gram_z_a, has, har, step).wait_send()
        for s, dc in pairs:
            gram_out_a(s, dc).wait_send()
    for s, dc in pairs:
        gram_b(s, dc).wait_send()
        gram_out_b(s, dc).wait_send()
    for step in Z_STEPS:
        gram_z_copy(gram_z_b, hbs, hbr, step).wait_send()


def sums(embeddings, start_basis):
    rows = embeddings.shape[0]
    dma = lambda *n: pltpu.SemaphoreType.DMA(n)
    vmem = pltpu.VMEM
    return pl.pallas_call(
        gather_kernel,
        out_shape=(
            jax.ShapeDtypeStruct((rows, K), F32),
            jax.ShapeDtypeStruct((NC, HALF, HALF), F32),
            jax.ShapeDtypeStruct((HALF, HALF), F32),
        ),
        in_specs=[pl.BlockSpec(memory_space=pl.ANY)] * 2,
        out_specs=(pl.BlockSpec(memory_space=pl.ANY),) + (pl.BlockSpec(memory_space=pltpu.VMEM),) * 2,
        scratch_shapes=[
            vmem((PARTS, rows, WIDE), F32),
            vmem((PARTS, rows, WIDE), BF16),
            vmem((PARTS, rows, WIDE), BF16),
            vmem((rows, K), F32),
            vmem((NC, HALVES, PLANE, 8, WIDE), F32),
            vmem((NC, HALVES, PLANE, 8, WIDE), F32),
            vmem((HALVES, PLANE, 8, OWN), F32),
            vmem((HALVES, PLANE - 1, 8, OWN), F32),
            vmem((HALVES, OWN_TILES, 8, 128), F32),
            vmem((NZ, 8, 128), F32),
            vmem((HALVES, PLANE, 8, D), F32),
            vmem((rows, K), F32),
            vmem((3, PLANE, 8, 128), F32),
            vmem((32, 8, 128), F32),
            vmem((32, 8, 128), F32),
            vmem((NZ, 8, 128), F32),
            vmem((NZ, 8, 128), F32),
            vmem((3, PLANE, 8, 128), F32),
            dma(PARTS + 1),
            dma(NC), dma(NC),
            dma(HALVES, PLANE), dma(HALVES, PLANE),
            dma(HALVES, OWN_TILES), dma(NZ),
            dma(NZ), dma(HALVES, OWN_TILES),
            dma(HALVES, PLANE), dma(HALVES, PLANE),
            dma(HALVES, PLANE), dma(HALVES, PLANE),
            dma(PLANE), dma(32),
            dma(32), dma(32),
            dma(NZ), dma(NZ),
            dma(NZ), dma(NZ),
            dma(32), dma(PLANE),
            dma(32), dma(NC, PLANE),
            pltpu.SemaphoreType.DMA,
        ],
        compiler_params=pltpu.CompilerParams(
            collective_id=0, has_side_effects=True, vmem_limit_bytes=VMEM_BYTES
        ),
        name="sums",
    )(embeddings, start_basis)


def factor_block(cols, strips, size):
    rows = lax.broadcasted_iota(jnp.int32, (size, 128), 0)
    scale = jnp.zeros((size, 128), F32)
    for j in range(0, size, 2):
        cj, cn = cols[j], cols[j + 1]
        a, b, d = cj[j:j + 1], cj[j + 1:j + 2], cn[j + 1:j + 2]
        q = 1.0 / (a * d - b * b)
        aq, bq, dq = a * q, b * q, d * q
        u = cj * dq - cn * bq
        v = cn * aq - cj * bq
        for k in range(j + 2, size):
            lo = (k // 8) * 8
            new = cols[k][lo:] - (u[lo:] * cj[k:k + 1] + v[lo:] * cn[k:k + 1])
            cols[k] = jnp.concatenate([cols[k][:lo], new], 0) if lo else new
        below = rows > j + 1
        ba = b * (1.0 / a)
        um = jnp.where(below, u, jnp.where(rows == j + 1, ba, 0.0))
        vm = jnp.where(below, v, 0.0)
        strips = [s - (um * s[j:j + 1] + vm * s[j + 1:j + 2]) for s in strips]
        ra = lax.rsqrt(a)
        rd = lax.rsqrt(d - ba * b)
        scale = jnp.where(rows == j, ra, jnp.where(rows == j + 1, rd, scale))
    return [s * scale for s in strips]


LEFT = (0, 0, 1, 0, 2, 1)
RIGHT = (0, 1, 0, 2, 0, 1)


def stacked(pieces, order):
    return jnp.concatenate([pieces[i] for i in order], 0)


def eliminate(panels):
    size = BLOCK
    done = []
    for k in range(HALF // size):
        off = k * size
        strips = [panel[:size] for panel in panels]
        cols = [jnp.broadcast_to(strips[0][:, off + j:off + j + 1], (size, 128)) for j in range(size)]
        strips = factor_block(cols, strips, size)
        done.append(strips[1:])
        if off + size == HALF:
            break
        pieces = [split3(s) for s in strips]
        left = stacked(pieces[0], LEFT)
        right = jnp.concatenate([stacked(piece, RIGHT) for piece in pieces], 1)
        change = mm(left, right, TN)
        panels = [
            panel[size:] - change[off + size:, 128 * i:128 * (i + 1)] for i, panel in enumerate(panels)
        ]
    return [jnp.concatenate([strips[i] for strips in done], 0) for i in range(len(panels) - 1)]


def mm6(a, b, dims):
    ah, am, al = split3(a)
    bh, bm, bl = split3(b)
    return mm(ah, bh, dims) + (mm(ah, bm, dims) + mm(am, bh, dims)) + (mm(am, bm, dims) + (mm(ah, bl, dims) + mm(al, bh, dims)))


def diagonal():
    return lax.broadcasted_iota(jnp.int32, (HALF, HALF), 0) == lax.broadcasted_iota(jnp.int32, (HALF, HALF), 1)


def diagonal_scales(value):
    entries = jnp.where(diagonal(), value, 0.0)
    return (
        lax.rsqrt(jnp.sum(entries, axis=1, keepdims=True)),
        lax.rsqrt(jnp.sum(entries, axis=0, keepdims=True)),
    )


def first_inverse(aa):
    col, row = diagonal_scales(aa)
    (inverse,) = eliminate([aa * col * row, jnp.where(diagonal(), 1.0, 0.0)])
    return inverse * row


def basis_kernel(scale, gram_ref, first_ref, image_hbm, out_ref, image, sem):
    copy = pltpu.make_async_copy(image_hbm, image, sem)
    copy.start()
    first = first_ref[...]
    ab, bb = gram_ref[0], gram_ref[1]
    col, row = diagonal_scales(bb)
    cross = mm6(first, ab * row, NN)
    turned = cross.T
    rest = bb * col * row - mm6(turned, cross, NN)
    lower = mm6(turned, first, NN)
    copy.wait()
    fh, fl = split2(first * scale)
    ih, il = split2(image[:, :HALF])
    out_ref[:, :HALF] = mm(ih, fh, NT) + (mm(ih, fl, NT) + mm(il, fh, NT))
    below, second = eliminate([rest, -lower, jnp.where(diagonal(), 1.0, 0.0)])
    gh, gl = split2(jnp.concatenate([below, second * row], 1) * scale)
    hi, lo = split2(image[...])
    out_ref[:, HALF:] = mm(hi, gh, NT) + (mm(hi, gl, NT) + mm(lo, gh, NT))


def basis_of(gram, first, image, scale):
    rows = image.shape[0]
    in_vmem = pl.BlockSpec(memory_space=pltpu.VMEM)
    return pl.pallas_call(
        functools.partial(basis_kernel, scale),
        out_shape=jax.ShapeDtypeStruct((rows, K), F32),
        in_specs=[in_vmem, in_vmem, pl.BlockSpec(memory_space=pl.ANY)],
        out_specs=in_vmem,
        scratch_shapes=[pltpu.VMEM((rows, K), F32), pltpu.SemaphoreType.DMA],
        compiler_params=pltpu.CompilerParams(vmem_limit_bytes=VMEM_BYTES),
        name="basis",
    )(gram, first, image)


def local(embeddings, start_basis):
    total_rows = embeddings.shape[0] * lax.axis_size("dp")
    image, gram, first = sums(embeddings, start_basis)
    return basis_of(gram, first, image, float(total_rows) ** 0.5)


def solution(mesh):
    in_specs = (P("dp", None), P("dp", None))
    out_specs = P("dp", None)
    return jax.shard_map(local, mesh=mesh, in_specs=in_specs, out_specs=out_specs, check_vma=False)
```

time: 1130 us -> 84 us (0.07)
  waiting for transfers between devices: 550 us -> 0 us
  other arithmetic: 396 us -> 0 us
  Pallas kernels: 0 us -> 83.6 us
  matrix products: 61.5 us -> 0 us
  starting transfers between devices: 44.7 us -> 0 us
  local copies, waits for them, and re-layouts: 41.9 us -> 0 us
  between operations: 26.8 us -> 0.17 us
    psum x1 -> x0, waiting for transfers between devices: 472 us -> none  [local(): sketch = lax.psum(partial_sketch, 'dp')]
    another operation x72 -> x0, other arithmetic: 375 us -> none  [the longest x63 317 us: local(): lower = jnp.linalg.cholesky(merged)]
    pallas_call x0 -> x2, Pallas kernels: none -> 83.6 us  [the longest x1 76.7 us: sums(): pl.pallas_call(gather_kernel, out_shape=(jax.ShapeDtypeStruct((rows, K),...]
    ppermute x9 -> x0, waiting for transfers between devices: 77.5 us -> none  [partner_2(): return lax.ppermute(value, axis, pairs)]
    ppermute x9 -> x0, starting transfers between devices: 44.7 us -> none  [partner_2(): return lax.ppermute(value, axis, pairs)]
    another operation x23 -> x0, matrix products: 31.3 us -> none  [the longest x18 25 us: local(): lower = jnp.linalg.cholesky(merged)]
    dot_general x21 -> x0, matrix products: 30.3 us -> none  [the longest x9 11 us: local(): jnp.dot(partner, partner.T, precision=lax.Precision.HIGHEST, preferred_el...]
    add x9 -> x0, local copies, waits for them, and re-layouts: 16 us -> none  [local(): jnp.dot(lower, lower.T, precision=lax.Precision.HIGHEST, preferred_elemen...]
  transfers between devices with their start and end apart: 10 -> 0, of which waited for: 10 -> 0; matrix products, arithmetic and copies ran while one was open for 0% -> 0% of each run, Pallas kernels for 0% -> 0%
where the time goes in v2:
time: 84 us; the launch traced here: 83.8 us
  Pallas kernels  83.6 us (100%)
    pallas_call x1, Pallas kernels, sums(): pl.pallas_call(gather_kernel, out_shape=(jax.ShapeDtypeStruct((rows, K),...  76.7 us
    pallas_call x1, Pallas kernels, basis_of(): pl.pallas_call(functools.partial(basis_kernel, scale), out_shape=jax.Shap...  6.91 us

profile of v2, /device:TPU:1, one launch (start us, length us, event | category | flops | bytes accessed | tf_op | source)
XLA Modules:
  0.0 83.8 jit_solution(6348514503158586523)
XLA Ops:
  0.0 76.7 %sums.1 = (f32[832,256]{1,0:T(8,128)}, f32[2,128,128]{2,1,0:T(8,128)}, f32[128,128]{1,0:T(8,128)}) custom-call(f32[832,1024]{1,0:T(8,128)} %emb_hbm.1, f32[832,256]{1,0:T(8,128)} %start_hbm.1), custom_call_target="tpu_custom_call" | custom-call | tf_op jit(solution)/shard_map/sums/pallas_call | solution.py:367
  76.7 6.9 %basis.1 = f32[832,256]{1,0:T(8,128)} custom-call(f32[2,128,128]{2,1,0:T(8,128)} %get-tuple-element.8.gram_ref, f32[128,128]{1,0:T(8,128)} %get-tuple-element.9.first_ref, f32[832,256]{1,0:T(8,128)} %get-tuple-element.10.image_hbm), custom_call_target="tpu_custom_call" | custom-call | tf_op jit(solution)/shard_map/basis/pallas_call | solution.py:518

commit v3 on v2

--- a/solution.py
+++ b/solution.py
@@ -72,7 +72,7 @@
     emb, emb_hi, emb_lo, start, give, core_in, part, plane_in, tiles, z_in, sketch,
     image, gram_part, gram_in_a, gram_in_b, gram_z_a, gram_z_b, gram_all,
     load_sem, core_s, core_r, xs, xr, zs, zr, ags, agr, bs, br, fs, fr,
-    gas, gar, gbs, gbr, has, har, hbs, hbr, kas, kar, kbs, kbr, out_sem,
+    gas, gar, gbs, gbr, has, har, hbs, hbr, kas, kar, kbs, kbr, out_sem, relay,
 ):
     me = lax.axis_index("dp")
     x, z, y, c = me // (NZ * NY * NC), (me // (NY * NC)) % NZ, (me // NC) % NY, me % NC
@@ -94,7 +94,7 @@
         copy.start()
 
     barrier = pltpu.get_barrier_semaphore()
-    greeted = [device(x, (z + step) % NZ, y, c) for step in Z_STEPS]
+    greeted = [device(x, (z + step) % NZ, y, c) for step in Z_STEPS if min(step, NZ - step) <= NZ // 4]
     greeted += [at(offset(x, y, dx, dy), (c + dc) % NC) for dx, dy, dc in PLANE_CORE_STEPS]
     for other in greeted:
         pl.semaphore_signal(barrier, inc=1, device_id={"dp": other}, device_id_type=pl.DeviceIdType.MESH)
@@ -116,6 +116,8 @@
             give[i] = total
             if i == 0:
                 pl.semaphore_wait(barrier, len(greeted))
+                for step in (NZ // 4, NZ - NZ // 4):
+                    pl.semaphore_signal(relay, inc=1, device_id={"dp": device(x, (z + step) % NZ, y, c)}, device_id_type=pl.DeviceIdType.MESH)
             core_copy(i).start()
         else:
             j = i - NC
@@ -129,6 +131,8 @@
     for h in range(HALVES):
         for o in range(PLANE - 1):
             plane_copy(h, o).start()
+
+    pl.semaphore_wait(relay, 2)
 
     def keeper(h, t):
         return 4 * t + NC * h + c
@@ -206,8 +210,9 @@
         for j in range(NC):
             i = (NC if core is c else 0) + j
             block = sketch[h, :, :, lanes(core * OWN + j * WIDE, WIDE)]
-            hi, lo = split2(block.reshape(PLANE * 8, WIDE))
-            term = mm(emb_hi[i], hi, NT) + (mm(emb_hi[i], lo, NT) + mm(emb_lo[i], hi, NT))
+            hi, lo = split2(block.reshape(HALF, WIDE))
+            both = mm(jnp.concatenate([hi, lo], 0), emb_hi[i], NT)
+            term = both[:HALF] + (both[HALF:] + mm(hi, emb_lo[i], NT))
             total = term if total is None else total + term
         return total
 
@@ -231,19 +236,18 @@
 
     pairs = [(s, dc) for s in range(PLANE) for dc in range(NC) if (s, dc) != (0, 0)]
 
-    turned = []
+    pieces = []
     for h in range(HALVES):
         for o in range(PLANE):
             block = block_of(h, source(o), 1 - c)
             remote(block, block, fs.at[h, o], fr.at[h, o], me).wait_recv()
-        value = halves[h] + image_part(h, 1 - c)
-        image[:, h * HALF:(h + 1) * HALF] = value
-        turned.append(split2(value.T))
-        bh, bl = split2(value)
+        halves[h] = halves[h] + image_part(h, 1 - c)
+        pieces += split2(halves[h])
+        gram = mm(jnp.concatenate(pieces[-2:], 0), jnp.concatenate(pieces, 0), NT)
+        gram = gram[:HALF] + gram[HALF:]
         for g in range(h + 1):
-            ah, al = turned[g]
-            gram = mm(ah, bh, NN) + (mm(ah, bl, NN) + mm(al, bh, NN)) + mm(al, bl, NN)
-            gram_part[h + g] = gram.reshape(PLANE, 8, 128)
+            block = gram[:, g * K:g * K + HALF] + gram[:, g * K + HALF:(g + 1) * K]
+            gram_part[h + g] = block.reshape(PLANE, 8, 128)
         if h == 0:
             for s in range(1, PLANE):
                 gram_a(s).start()
@@ -254,8 +258,6 @@
         else:
             for s, dc in pairs:
                 gram_b(s, dc).start()
-    image_copy = pltpu.make_async_copy(image, image_hbm, out_sem)
-    image_copy.start()
 
     def gram_z_copy(store, send, recv, step):
         return remote(store.at[z], store.at[z], send.at[step], recv.at[step], device(x, (z + step) % NZ, y, c))
@@ -280,49 +282,9 @@
     for step in Z_STEPS:
         gram_z_copy(gram_z_b, hbs, hbr, step).start()
 
-    def z_sum(store, send, recv):
-        for step in reversed(Z_STEPS):
-            src = (z - step + NZ) % NZ
-            remote(store.at[src], store.at[src], send.at[step], recv.at[step], me).wait_recv()
-        total = store[0]
-        for i in range(1, NZ):
-            total = total + store[i]
-        return total
-
-    def gram_out_a(s, dc):
-        block = gram_all.at[0, p]
-        return remote(block, block, kas.at[NC * s + dc], kar.at[p], at(offset(x, y, *around[s]), (c + dc) % NC))
-
-    def gram_out_b(s, dc):
-        block = gram_all.at[1 + c, p]
-        return remote(block, block, kbs.at[NC * s + dc], kbr.at[c, p], at(offset(x, y, *around[s]), (c + dc) % NC))
-
-    @pl.when(keeps_a)
-    def _():
-        gram_all[0, p] = z_sum(gram_z_a, has, har)
-        for s, dc in pairs:
-            gram_out_a(s, dc).start()
-
-    gram_all[1 + c, p] = z_sum(gram_z_b, hbs, hbr)
-    for s, dc in pairs:
-        gram_out_b(s, dc).start()
-
-    for s in range(1, PLANE):
-        q = offset(x, y, *around[s])
-        remote(gram_all.at[0, q], gram_all.at[0, q], kas.at[0], kar.at[q], me).wait_recv()
-
-    @pl.when(jnp.logical_not(keeps_a))
-    def _():
-        remote(gram_all.at[0, p], gram_all.at[0, p], kas.at[0], kar.at[p], me).wait_recv()
-
-    first_ref[...] = first_inverse(gram_all[0].reshape(HALF, HALF))
-
-    for s, dc in pairs:
-        q, core = offset(x, y, *around[s]), (c + dc) % NC
-        remote(gram_all.at[1 + core, q], gram_all.at[1 + core, q], kbs.at[0], kbr.at[core, q], me).wait_recv()
-    gram_ref[...] = gram_all[1:3].reshape(NC, HALF, HALF)
-
-    image_copy.wait()
+    image[...] = jnp.concatenate(halves, 0).T
+    image_copy = pltpu.make_async_copy(image, image_hbm, out_sem)
+    image_copy.start()
     for i in range(NC):
         core_copy(i).wait_send()
     for h in range(HALVES):
@@ -347,17 +309,63 @@
     def _():
         gram_a(0).wait_send()
 
+    for s, dc in pairs:
+        gram_b(s, dc).wait_send()
+
+    def z_sum(store, send, recv):
+        for step in reversed(Z_STEPS):
+            src = (z - step + NZ) % NZ
+            remote(store.at[src], store.at[src], send.at[step], recv.at[step], me).wait_recv()
+        total = store[0]
+        for i in range(1, NZ):
+            total = total + store[i]
+        return total
+
+    def gram_out_a(s, dc):
+        block = gram_all.at[0, p]
+        return remote(block, block, kas.at[NC * s + dc], kar.at[p], at(offset(x, y, *around[s]), (c + dc) % NC))
+
+    def gram_out_b(s, dc):
+        block = gram_all.at[1 + c, p]
+        return remote(block, block, kbs.at[NC * s + dc], kbr.at[c, p], at(offset(x, y, *around[s]), (c + dc) % NC))
+
+    @pl.when(keeps_a)
+    def _():
+        gram_all[0, p] = z_sum(gram_z_a, has, har)
+        for s, dc in pairs:
+            gram_out_a(s, dc).start()
+
+    gram_all[1 + c, p] = z_sum(gram_z_b, hbs, hbr)
+    for s, dc in pairs:
+        gram_out_b(s, dc).start()
+
+    for s in range(1, PLANE):
+        q = offset(x, y, *around[s])
+        remote(gram_all.at[0, q], gram_all.at[0, q], kas.at[0], kar.at[q], me).wait_recv()
+
+    @pl.when(jnp.logical_not(keeps_a))
+    def _():
+        remote(gram_all.at[0, p], gram_all.at[0, p], kas.at[0], kar.at[p], me).wait_recv()
+
+    first_ref[...] = first_inverse(gram_all[0].reshape(HALF, HALF))
+
     @pl.when(keeps_a)
     def _():
         for step in Z_STEPS:
             gram_z_copy(gram_z_a, has, har, step).wait_send()
         for s, dc in pairs:
             gram_out_a(s, dc).wait_send()
-    for s, dc in pairs:
-        gram_b(s, dc).wait_send()
-        gram_out_b(s, dc).wait_send()
+
     for step in Z_STEPS:
         gram_z_copy(gram_z_b, hbs, hbr, step).wait_send()
+    for s, dc in pairs:
+        gram_out_b(s, dc).wait_send()
+    image_copy.wait()
+
+    for s, dc in pairs:
+        q, core = offset(x, y, *around[s]), (c + dc) % NC
+        remote(gram_all.at[1 + core, q], gram_all.at[1 + core, q], kbs.at[0], kbr.at[core, q], me).wait_recv()
+    gram_ref[...] = gram_all[1:3].reshape(NC, HALF, HALF)
 
 
 def sums(embeddings, start_basis):
@@ -406,6 +414,7 @@
             dma(32), dma(PLANE),
             dma(32), dma(NC, PLANE),
             pltpu.SemaphoreType.DMA,
+            pltpu.SemaphoreType.REGULAR,
         ],
         compiler_params=pltpu.CompilerParams(
             collective_id=0, has_side_effects=True, vmem_limit_bytes=VMEM_BYTES
@@ -496,12 +505,11 @@
     copy = pltpu.make_async_copy(image_hbm, image, sem)
     copy.start()
     first = first_ref[...]
-    ab, bb = gram_ref[0], gram_ref[1]
+    ba, bb = gram_ref[0], gram_ref[1]
     col, row = diagonal_scales(bb)
-    cross = mm6(first, ab * row, NN)
-    turned = cross.T
-    rest = bb * col * row - mm6(turned, cross, NN)
-    lower = mm6(turned, first, NN)
+    cross = mm6(ba * col, first, NT)
+    rest = bb * col * row - mm6(cross, cross, NT)
+    lower = mm6(cross, first, NN)
     copy.wait()
     fh, fl = split2(first * scale)
     ih, il = split2(image[:, :HALF])

time: 84 us -> 81 us (0.964)
  Pallas kernels: 83.6 us -> 80.6 us
    pallas_call x1, Pallas kernels: 76.7 us -> 73.7 us  [sums(): pl.pallas_call(gather_kernel, out_shape=(jax.ShapeDtypeStruct((rows, K),...]
where the time goes in v3:
time: 81 us; the launch traced here: 80.8 us
  Pallas kernels  80.6 us (100%)
    pallas_call x1, Pallas kernels, sums(): pl.pallas_call(gather_kernel, out_shape=(jax.ShapeDtypeStruct((rows, K),...  73.7 us
    pallas_call x1, Pallas kernels, basis_of(): pl.pallas_call(functools.partial(basis_kernel, scale), out_shape=jax.Shap...  6.91 us

profile of v3, /device:TPU:1, one launch (start us, length us, event | category | flops | bytes accessed | tf_op | source)
XLA Modules:
  0.0 80.8 jit_solution(13563319029565908959)
XLA Ops:
  0.0 73.7 %sums.1 = (f32[832,256]{1,0:T(8,128)}, f32[2,128,128]{2,1,0:T(8,128)}, f32[128,128]{1,0:T(8,128)}) custom-call(f32[832,1024]{1,0:T(8,128)} %emb_hbm.1, f32[832,256]{1,0:T(8,128)} %start_hbm.1), custom_call_target="tpu_custom_call" | custom-call | tf_op jit(solution)/shard_map/sums/pallas_call | solution.py:375
  73.7 6.9 %basis.1 = f32[832,256]{1,0:T(8,128)} custom-call(f32[2,128,128]{2,1,0:T(8,128)} %get-tuple-element.8.gram_ref, f32[128,128]{1,0:T(8,128)} %get-tuple-element.9.first_ref, f32[832,256]{1,0:T(8,128)} %get-tuple-element.10.image_hbm), custom_call_target="tpu_custom_call" | custom-call | tf_op jit(solution)/shard_map/basis/pallas_call | solution.py:526

commit v4 on v3

v4 whole, which is shorter than its diff:
```python
import functools

import jax
import jax.numpy as jnp
from jax import lax
from jax.experimental import pallas as pl
from jax.experimental.pallas import tpu as pltpu
from jax.sharding import PartitionSpec as P

F32, BF16 = jnp.float32, jnp.bfloat16
NX, NZ, NY, NC = 4, 16, 4, 2
PLANE = NX * NY
D, K = 1024, 256
PARTS = 4
WIDE = D // PARTS
HALVES = 2
HALF = K // HALVES
OWN = D // NC
OWN_TILES = OWN // 128
BLOCK = 16
VMEM_BYTES = 60 << 20

PLANE_STEPS = sorted(
    [(dx, dy) for dx in range(NX) for dy in range(NY) if (dx, dy) != (0, 0)],
    key=lambda s: -(min(s[0], NX - s[0]) + min(s[1], NY - s[1])),
)
PLANE_CORE_STEPS = [(dx, dy, dc) for dx, dy in PLANE_STEPS for dc in range(NC)] + [(0, 0, 1)]
Z_STEPS = sorted(range(1, NZ), key=lambda d: -min(d, NZ - d))

NT = (((1,), (1,)), ((), ()))
NN = (((1,), (0,)), ((), ()))
TN = (((0,), (0,)), ((), ()))


def mm(a, b, dims):
    return lax.dot_general(a, b, dims, preferred_element_type=F32)


def split2(value):
    high = value.astype(BF16)
    return high, (value - high.astype(F32)).astype(BF16)


def split3(value):
    high = value.astype(BF16)
    rest = value - high.astype(F32)
    middle = rest.astype(BF16)
    return high, middle, (rest - middle.astype(F32)).astype(BF16)


def device(x, z, y, c):
    return ((x * NZ + z) * NY + y) * NC + c


def remote(src, dst, send, recv, target):
    return pltpu.make_async_remote_copy(
        src_ref=src,
        dst_ref=dst,
        send_sem=send,
        recv_sem=recv,
        device_id={"dp": target},
        device_id_type=pl.DeviceIdType.MESH,
    )


def offset(x, y, dx, dy):
    return ((x + dx) % NX) * NY + (y + dy) % NY


def landed(ref, sem):
    pltpu.make_async_copy(ref, ref, sem).wait()


def gather_kernel(
    emb_hbm, start_hbm, image_hbm, gram_ref, first_ref,
    emb, emb_hi, emb_lo, start, give, core_in, part, plane_in, tiles, z_in, sketch,
    image, gram_part, gram_in_a, gram_in_b, gram_z_a, gram_z_b, gram_all,
    load_sem, core_s, core_r, xs, xr, zs, zr, ags, agr, bs, br, fs, fr,
    gas, gar, gbs, gbr, has, har, hbs, hbr, kas, kar, kbs, kbr, out_sem, relay,
):
    me = lax.axis_index("dp")
    x, z, y, c = me // (NZ * NY * NC), (me // (NY * NC)) % NZ, (me // NC) % NY, me % NC
    p = x * NY + y
    sibling = device(x, z, y, 1 - c)
    around = [(0, 0)] + PLANE_STEPS

    def at(q, core):
        return device(q // NY, z, q % NY, core)

    places = [NC * (1 - c), NC * (1 - c) + 1, NC * c, NC * c + 1]

    def wide(i):
        return pl.ds(pl.multiple_of(places[i] * WIDE, WIDE), WIDE)

    loads = [pltpu.make_async_copy(start_hbm, start, load_sem.at[PARTS])]
    loads += [pltpu.make_async_copy(emb_hbm.at[:, wide(i)], emb.at[i], load_sem.at[i]) for i in range(PARTS)]
    for copy in loads:
        copy.start()

    barrier = pltpu.get_barrier_semaphore()
    greeted = [device(x, (z + step) % NZ, y, c) for step in Z_STEPS if min(step, NZ - step) <= NZ // 4]
    greeted += [at(offset(x, y, dx, dy), (c + dc) % NC) for dx, dy, dc in PLANE_CORE_STEPS]
    for other in greeted:
        pl.semaphore_signal(barrier, inc=1, device_id={"dp": other}, device_id_type=pl.DeviceIdType.MESH)

    loads[0].wait()
    start_hi, start_lo = split2(start[...].T)

    for i in range(PARTS):
        loads[1 + i].wait()
        hi, lo = split2(emb[i])
        emb_hi[i] = hi
        emb_lo[i] = lo
        total = mm(start_hi, hi, NN) + (mm(start_hi, lo, NN) + mm(start_lo, hi, NN))
        store, j = (give, i) if i < NC else (part, i - NC)
        store[:, :, :, j * WIDE:(j + 1) * WIDE] = total.reshape(HALVES, PLANE, 8, WIDE)

    pl.semaphore_wait(barrier, len(greeted))
    for step in (NZ // 4, NZ - NZ // 4):
        pl.semaphore_signal(relay, inc=1, device_id={"dp": device(x, (z + step) % NZ, y, c)}, device_id_type=pl.DeviceIdType.MESH)

    def core_copy(h):
        return remote(give.at[h], core_in.at[h], core_s.at[h], core_r.at[h], sibling)

    def plane_copy(h, o):
        q = offset(x, y, *PLANE_STEPS[o])
        return remote(part.at[h, q], plane_in.at[h, o], xs.at[h], xr.at[h], at(q, c))

    for h in range(HALVES):
        core_copy(h).start()
    for h in range(HALVES):
        core_copy(h).wait_recv()
        part[h] = part[h] + core_in[h]
        for o in range(PLANE - 1):
            plane_copy(h, o).start()

    pl.semaphore_wait(relay, 2)

    def keeper(h, t):
        return 4 * t + NC * h + c

    def z_copy(h, t):
        step = (keeper(h, t) - z + NZ) % NZ
        return remote(tiles.at[h, t], z_in.at[step], zs.at[h, t], zr.at[0], device(x, keeper(h, t), y, c))

    for h in range(HALVES):
        landed(plane_in.at[h], xr.at[h])
        total = part[h, p]
        for o in range(PLANE - 1):
            total = total + plane_in[h, o]
        for t in range(OWN_TILES):
            tiles[h, t] = total[:, t * 128:(t + 1) * 128]
        for t in range(OWN_TILES):
            @pl.when(keeper(h, t) != z)
            def _(h=h, t=t):
                z_copy(h, t).start()

    def lanes(start, size):
        return pl.ds(pl.multiple_of(start, 128), size)

    def tile_of(h, t):
        return sketch.at[h, p, :, lanes(c * OWN + t * 128, 128)]

    mine = z // 4

    def z_out(h, step):
        return remote(tile_of(h, mine), tile_of(h, mine), ags.at[0], agr.at[h, mine], device(x, (z + step) % NZ, y, c))

    def keeps(h):
        return z % 4 == NC * h + c

    for h in range(HALVES):
        @pl.when(keeps(h))
        def _(h=h):
            landed(z_in.at[pl.ds(1, NZ - 1)], zr.at[0])
            total = tiles[h, mine]
            for step in range(1, NZ):
                total = total + z_in[step]
            sketch[h, p, :, lanes(c * OWN + mine * 128, 128)] = total
            for step in Z_STEPS:
                z_out(h, step).start()

    def block_of(h, q, core):
        return sketch.at[h, q, :, lanes(core * OWN, OWN)]

    def plane_out(h, o):
        q = offset(x, y, *PLANE_STEPS[o])
        return remote(block_of(h, p, c), block_of(h, p, c), bs.at[h], br.at[h, o], at(q, c))

    def source(o):
        if o == PLANE - 1:
            return p
        dx, dy = PLANE_STEPS[o]
        return offset(x, y, -dx, -dy)

    def forward(h, o):
        return remote(block_of(h, source(o), c), block_of(h, source(o), c), fs.at[h], fr.at[h], sibling)

    for h in range(HALVES):
        for t in range(OWN_TILES):
            @pl.when(keeper(h, t) != z)
            def _(h=h, t=t):
                landed(tile_of(h, t), agr.at[h, t])
        for o in range(PLANE - 1):
            plane_out(h, o).start()
        forward(h, PLANE - 1).start()

    def image_part(h, core):
        total = None
        for j in range(NC):
            i = (NC if core is c else 0) + j
            block = sketch[h, :, :, lanes(core * OWN + j * WIDE, WIDE)]
            hi, lo = split2(block.reshape(HALF, WIDE))
            both = mm(jnp.concatenate([hi, lo], 0), emb_hi[i], NT)
            term = both[:HALF] + (both[HALF:] + mm(hi, emb_lo[i], NT))
            total = term if total is None else total + term
        return total

    halves = []
    for h in range(HALVES):
        for o in reversed(range(PLANE - 1)):
            block = block_of(h, source(o), c)
            landed(block, br.at[h, o])
            forward(h, o).start()
        halves.append(image_part(h, c))

    keeps_a = y % NC == c

    pairs = [(s, dc) for s in range(PLANE) for dc in range(NC) if (s, dc) != (0, 0)]

    def gram_a(s):
        q = offset(x, y, *around[s])
        slot = NC * s + ((q % NY) + c) % NC
        return remote(gram_part.at[0, q], gram_in_a.at[slot], gas.at[s], gar.at[0], at(q, (q % NY) % NC))

    def gram_b(s, dc):
        q, core = offset(x, y, *around[s]), (c + dc) % NC
        return remote(gram_part.at[1 + core, q], gram_in_b.at[NC * s + dc], gbs.at[0], gbr.at[0], at(q, core))

    pieces = []
    for h in range(HALVES):
        landed(part.at[h], fr.at[h])
        halves[h] = halves[h] + image_part(h, 1 - c)
        pieces += split2(halves[h])
        gram = mm(jnp.concatenate(pieces[-2:], 0), jnp.concatenate(pieces, 0), NT)
        gram = gram[:HALF] + gram[HALF:]
        for g in range(h + 1):
            block = gram[:, g * K:g * K + HALF] + gram[:, g * K + HALF:(g + 1) * K]
            gram_part[h + g] = block.reshape(PLANE, 8, 128)
        if h == 0:
            for s in range(1, PLANE):
                gram_a(s).start()

            @pl.when(jnp.logical_not(keeps_a))
            def _():
                gram_a(0).start()
        else:
            for s, dc in pairs:
                gram_b(s, dc).start()

    def gram_z_copy(store, send, recv, step):
        return remote(store.at[z], store.at[z], send.at[0], recv.at[0], device(x, (z + step) % NZ, y, c))

    @pl.when(keeps_a)
    def _():
        total = gram_part[0, p]
        landed(gram_in_a.at[pl.ds(1, 31)], gar.at[0])
        for slot in range(1, 32):
            total = total + gram_in_a[slot]
        gram_z_a[z] = total
        for step in Z_STEPS:
            gram_z_copy(gram_z_a, has, har, step).start()

    total = gram_part[1 + c, p]
    landed(gram_in_b.at[pl.ds(1, 31)], gbr.at[0])
    for slot in range(1, 32):
        total = total + gram_in_b[slot]
    gram_z_b[z] = total
    for step in Z_STEPS:
        gram_z_copy(gram_z_b, hbs, hbr, step).start()

    image[...] = jnp.concatenate(halves, 0).T
    image_copy = pltpu.make_async_copy(image, image_hbm, out_sem)
    image_copy.start()
    for h in range(HALVES):
        core_copy(h).wait_send()
        landed(plane_in.at[h], xs.at[h])
        landed(plane_in.at[h], bs.at[h])
        landed(part.at[h], fs.at[h])
        for t in range(OWN_TILES):
            @pl.when(keeper(h, t) != z)
            def _(h=h, t=t):
                z_copy(h, t).wait_send()

        @pl.when(keeps(h))
        def _():
            landed(z_in.at[pl.ds(1, NZ - 1)], ags.at[0])
    for s in range(1, PLANE):
        gram_a(s).wait_send()

    @pl.when(jnp.logical_not(keeps_a))
    def _():
        gram_a(0).wait_send()

    landed(gram_in_b.at[pl.ds(1, 31)], gbs.at[0])

    def z_sum(store, recv):
        landed(store.at[pl.ds(0, NZ - 1)], recv.at[0])
        total = store[0]
        for i in range(1, NZ):
            total = total + store[i]
        return total

    def gram_out_a(s, dc):
        block = gram_all.at[0, p]
        return remote(block, block, kas.at[0], kar.at[0], at(offset(x, y, *around[s]), (c + dc) % NC))

    def gram_out_b(s, dc):
        block = gram_all.at[1 + c, p]
        return remote(block, block, kbs.at[0], kbr.at[0], at(offset(x, y, *around[s]), (c + dc) % NC))

    @pl.when(keeps_a)
    def _():
        gram_all[0, p] = z_sum(gram_z_a, har)
        for s, dc in pairs:
            gram_out_a(s, dc).start()

    gram_all[1 + c, p] = z_sum(gram_z_b, hbr)
    for s, dc in pairs:
        gram_out_b(s, dc).start()

    @pl.when(keeps_a)
    def _():
        landed(gram_all.at[0, pl.ds(0, PLANE - 1)], kar.at[0])

    @pl.when(jnp.logical_not(keeps_a))
    def _():
        landed(gram_all.at[0], kar.at[0])

    first_ref[...] = first_inverse(gram_all[0].reshape(HALF, HALF))

    @pl.when(keeps_a)
    def _():
        landed(gram_z_a.at[pl.ds(0, NZ - 1)], has.at[0])
        landed(gram_in_a.at[pl.ds(1, 31)], kas.at[0])

    landed(gram_z_b.at[pl.ds(0, NZ - 1)], hbs.at[0])
    landed(gram_in_b.at[pl.ds(1, 31)], kbs.at[0])
    image_copy.wait()

    landed(gram_in_b.at[pl.ds(1, 31)], kbr.at[0])
    gram_ref[...] = gram_all[1:3].reshape(NC, HALF, HALF)


def sums(embeddings, start_basis):
    rows = embeddings.shape[0]
    dma = lambda *n: pltpu.SemaphoreType.DMA(n)
    vmem = pltpu.VMEM
    return pl.pallas_call(
        gather_kernel,
        out_shape=(
            jax.ShapeDtypeStruct((rows, K), F32),
            jax.ShapeDtypeStruct((NC, HALF, HALF), F32),
            jax.ShapeDtypeStruct((HALF, HALF), F32),
        ),
        in_specs=[pl.BlockSpec(memory_space=pl.ANY)] * 2,
        out_specs=(pl.BlockSpec(memory_space=pl.ANY),) + (pl.BlockSpec(memory_space=pltpu.VMEM),) * 2,
        scratch_shapes=[
            vmem((PARTS, rows, WIDE), F32),
            vmem((PARTS, rows, WIDE), BF16),
            vmem((PARTS, rows, WIDE), BF16),
            vmem((rows, K), F32),
            vmem((HALVES, PLANE, 8, OWN), F32),
            vmem((HALVES, PLANE, 8, OWN), F32),
            vmem((HALVES, PLANE, 8, OWN), F32),
            vmem((HALVES, PLANE - 1, 8, OWN), F32),
            vmem((HALVES, OWN_TILES, 8, 128), F32),
            vmem((NZ, 8, 128), F32),
            vmem((HALVES, PLANE, 8, D), F32),
            vmem((rows, K), F32),
            vmem((3, PLANE, 8, 128), F32),
            vmem((32, 8, 128), F32),
            vmem((32, 8, 128), F32),
            vmem((NZ, 8, 128), F32),
            vmem((NZ, 8, 128), F32),
            vmem((3, PLANE, 8, 128), F32),
            dma(PARTS + 1),
            dma(HALVES), dma(HALVES),
            dma(HALVES), dma(HALVES),
            dma(HALVES, OWN_TILES), dma(1),
            dma(1), dma(HALVES, OWN_TILES),
            dma(HALVES), dma(HALVES, PLANE),
            dma(HALVES), dma(HALVES),
            dma(PLANE), dma(1),
            dma(1), dma(1),
            dma(1), dma(1),
            dma(1), dma(1),
            dma(1), dma(1),
            dma(1), dma(1),
            pltpu.SemaphoreType.DMA,
            pltpu.SemaphoreType.REGULAR,
        ],
        compiler_params=pltpu.CompilerParams(
            collective_id=0, has_side_effects=True, vmem_limit_bytes=VMEM_BYTES
        ),
        name="sums",
    )(embeddings, start_basis)


LEFT = (0, 0, 1, 0, 2, 1)
RIGHT = (0, 1, 0, 2, 0, 1)


def stacked(pieces, order):
    return jnp.concatenate([pieces[i] for i in order], 0)


def spread(block, size):
    return [jnp.broadcast_to(block[:, j:j + 1], (size, 128)) for j in range(size)]


def eliminate(panels):
    size = BLOCK
    rows = lax.broadcasted_iota(jnp.int32, (size, 128), 0)
    done = []
    strips = [panel[:size] for panel in panels]
    rest = [panel[size:] for panel in panels]
    for off in range(0, HALF, size):
        last = off + size == HALF
        cols = spread(strips[0][:, off:off + size], size)
        if not last:
            ahead = spread(strips[0][:, off + size:off + 2 * size].T, size)
            change = [0.0] * len(strips)
        scale = jnp.zeros((size, 128), F32)
        for j in range(0, size, 2):
            cj, cn = cols[j], cols[j + 1]
            a, b, d = cj[j:j + 1], cj[j + 1:j + 2], cn[j + 1:j + 2]
            q = 1.0 / (a * d - b * b)
            aq, bq, dq = a * q, b * q, d * q
            u = cj * dq - cn * bq
            v = cn * aq - cj * bq
            for k in range(j + 2, size):
                lo = (k // 8) * 8
                new = cols[k][lo:] - (u[lo:] * cj[k:k + 1] + v[lo:] * cn[k:k + 1])
                cols[k] = jnp.concatenate([cols[k][:lo], new], 0) if lo else new
            if not last:
                aj, an = ahead[j], ahead[j + 1]
                au = aj * dq - an * bq
                av = an * aq - aj * bq
                for k in range(j + 2, size):
                    ahead[k] = ahead[k] - (au * cj[k:k + 1] + av * cn[k:k + 1])
                change = [t + (au * s[j:j + 1] + av * s[j + 1:j + 2]) for t, s in zip(change, strips)]
            below = rows > j + 1
            ba = b * (1.0 / a)
            um = jnp.where(below, u, jnp.where(rows == j + 1, ba, 0.0))
            vm = jnp.where(below, v, 0.0)
            strips = [s - (um * s[j:j + 1] + vm * s[j + 1:j + 2]) for s in strips]
            ra = lax.rsqrt(a)
            rd = lax.rsqrt(d - ba * b)
            scale = jnp.where(rows == j, ra, jnp.where(rows == j + 1, rd, scale))
        strips = [s * scale for s in strips]
        done.append(strips[1:])
        if last:
            break
        following = [r[:size] - t for r, t in zip(rest, change)]
        behind = off + 2 * size
        if behind < HALF:
            pieces = [split3(s) for s in strips]
            left = stacked(pieces[0], LEFT)
            right = jnp.concatenate([stacked(piece, RIGHT) for piece in pieces], 1)
            product = mm(left, right, TN)[behind:]
            rest = [r[size:] - product[:, 128 * i:128 * (i + 1)] for i, r in enumerate(rest)]
        strips = following
    return [jnp.concatenate([strips[i] for strips in done], 0) for i in range(len(panels) - 1)]


def mm6(a, b, dims):
    ah, am, al = split3(a)
    bh, bm, bl = split3(b)
    return mm(ah, bh, dims) + (mm(ah, bm, dims) + mm(am, bh, dims)) + (mm(am, bm, dims) + (mm(ah, bl, dims) + mm(al, bh, dims)))


def diagonal():
    return lax.broadcasted_iota(jnp.int32, (HALF, HALF), 0) == lax.broadcasted_iota(jnp.int32, (HALF, HALF), 1)


def diagonal_scales(value):
    entries = jnp.where(diagonal(), value, 0.0)
    return (
        lax.rsqrt(jnp.sum(entries, axis=1, keepdims=True)),
        lax.rsqrt(jnp.sum(entries, axis=0, keepdims=True)),
    )


def first_inverse(aa):
    col, row = diagonal_scales(aa)
    (inverse,) = eliminate([aa * col * row, jnp.where(diagonal(), 1.0, 0.0)])
    return inverse * row


def basis_kernel(scale, gram_ref, first_ref, image_hbm, out_hbm, image, out, sems):
    copy = pltpu.make_async_copy(image_hbm, image, sems.at[0])
    copy.start()
    first = first_ref[...]
    ba, bb = gram_ref[0], gram_ref[1]
    col, row = diagonal_scales(bb)
    cross = mm6(ba * col, first, NT)
    rest = bb * col * row - mm6(cross, cross, NT)
    lower = mm6(cross, first, NN)
    copy.wait()
    rows = image.shape[0]
    outs = []

    def product(value, factor):
        hi, lo = split2(value)
        high, low = split2(factor)
        both = mm(hi, jnp.concatenate([high, low], 0), NT)
        return both[:, :HALF] + (both[:, HALF:] + mm(lo, high, NT))

    def leave(r, n, cols):
        outs.append(pltpu.make_async_copy(out.at[pl.ds(r, n), cols], out_hbm.at[pl.ds(r, n), cols], sems.at[1 + len(outs)]))
        outs[-1].start()

    out[:, :HALF] = product(image[:, :HALF], first * scale)
    leave(0, rows, pl.ds(0, HALF))
    below, second = eliminate([rest, -lower, jnp.where(diagonal(), 1.0, 0.0)])
    factor = jnp.concatenate([below, second * row], 1) * scale
    step = rows // 2
    for r in range(0, rows, step):
        out[r:r + step, HALF:] = product(image[r:r + step, :], factor)
        leave(r, step, pl.ds(HALF, HALF))
    for copy in outs:
        copy.wait()


def basis_of(gram, first, image, scale):
    rows = image.shape[0]
    in_vmem = pl.BlockSpec(memory_space=pltpu.VMEM)
    return pl.pallas_call(
        functools.partial(basis_kernel, scale),
        out_shape=jax.ShapeDtypeStruct((rows, K), F32),
        in_specs=[in_vmem, in_vmem, pl.BlockSpec(memory_space=pl.ANY)],
        out_specs=pl.BlockSpec(memory_space=pl.ANY),
        scratch_shapes=[pltpu.VMEM((rows, K), F32), pltpu.VMEM((rows, K), F32), pltpu.SemaphoreType.DMA((4,))],
        compiler_params=pltpu.CompilerParams(vmem_limit_bytes=VMEM_BYTES),
        name="basis",
    )(gram, first, image)


def local(embeddings, start_basis):
    total_rows = embeddings.shape[0] * lax.axis_size("dp")
    image, gram, first = sums(embeddings, start_basis)
    return basis_of(gram, first, image, float(total_rows) ** 0.5)


def solution(mesh):
    in_specs = (P("dp", None), P("dp", None))
    out_specs = P("dp", None)
    return jax.shard_map(local, mesh=mesh, in_specs=in_specs, out_specs=out_specs, check_vma=False)
```

time: 81 us -> 75.1 us (0.927)
  Pallas kernels: 80.6 us -> 74.7 us
    pallas_call x1, Pallas kernels: 73.7 us -> 68.6 us  [sums(): pl.pallas_call(gather_kernel, out_shape=(jax.ShapeDtypeStruct((rows, K),...]
    pallas_call x1, Pallas kernels: 6.91 us -> 6.07 us  [basis_of(): pl.pallas_call(functools.partial(basis_kernel, scale), out_shape=jax.Shap...]
where the time goes in v4:
time: 75.1 us; the launch traced here: 74.9 us
  Pallas kernels  74.7 us (99%)
    pallas_call x1, Pallas kernels, sums(): pl.pallas_call(gather_kernel, out_shape=(jax.ShapeDtypeStruct((rows, K),...  68.6 us
    pallas_call x1, Pallas kernels, basis_of(): pl.pallas_call(functools.partial(basis_kernel, scale), out_shape=jax.Shap...  6.07 us

profile of v4, /device:TPU:1, one launch (start us, length us, event | category | flops | bytes accessed | tf_op | source)
XLA Modules:
  0.0 74.9 jit_solution(5690097369190563163)
XLA Ops:
  0.0 68.6 %sums.1 = (f32[832,256]{1,0:T(8,128)}, f32[2,128,128]{2,1,0:T(8,128)}, f32[128,128]{1,0:T(8,128)}) custom-call(f32[832,1024]{1,0:T(8,128)} %emb_hbm.1, f32[832,256]{1,0:T(8,128)} %start_hbm.1), custom_call_target="tpu_custom_call" | custom-call | tf_op jit(solution)/shard_map/sums/pallas_call | solution.py:359
  68.7 6.1 %basis.1 = f32[832,256]{1,0:T(8,128)} custom-call(f32[2,128,128]{2,1,0:T(8,128)} %get-tuple-element.8.gram_ref, f32[128,128]{1,0:T(8,128)} %get-tuple-element.9.first_ref, f32[832,256]{1,0:T(8,128)} %get-tuple-element.10.image_hbm), custom_call_target="tpu_custom_call" | custom-call | tf_op jit(solution)/shard_map/basis/pallas_call | solution.py:539

commit v5 on v4

--- a/solution.py
+++ b/solution.py
@@ -63,8 +63,12 @@
     )
 
 
+def mod(value, n):
+    return lax.rem(value, n)
+
+
 def offset(x, y, dx, dy):
-    return ((x + dx) % NX) * NY + (y + dy) % NY
+    return mod(x + dx % NX, NX) * NY + mod(y + dy % NY, NY)
 
 
 def landed(ref, sem):
@@ -72,20 +76,20 @@
 
 
 def gather_kernel(
-    emb_hbm, start_hbm, image_hbm, gram_ref, first_ref,
+    emb_hbm, start_hbm, image_hbm, gram_hbm, first_hbm,
     emb, emb_hi, emb_lo, start, give, core_in, part, plane_in, tiles, z_in, sketch,
-    image, gram_part, gram_in_a, gram_in_b, gram_z_a, gram_z_b, gram_all,
+    image, gram_part, gram_in_a, gram_in_b, gram_z_a, gram_z_b, gram_a_all, gram_b_own, first,
     load_sem, core_s, core_r, xs, xr, zs, zr, ags, agr, bs, br, fs, fr,
     gas, gar, gbs, gbr, has, har, hbs, hbr, kas, kar, kbs, kbr, out_sem, relay,
 ):
     me = lax.axis_index("dp")
-    x, z, y, c = me // (NZ * NY * NC), (me // (NY * NC)) % NZ, (me // NC) % NY, me % NC
+    x, z, y, c = lax.div(me, NZ * NY * NC), mod(lax.div(me, NY * NC), NZ), mod(lax.div(me, NC), NY), mod(me, NC)
     p = x * NY + y
     sibling = device(x, z, y, 1 - c)
     around = [(0, 0)] + PLANE_STEPS
 
     def at(q, core):
-        return device(q // NY, z, q % NY, core)
+        return device(lax.div(q, NY), z, mod(q, NY), core)
 
     places = [NC * (1 - c), NC * (1 - c) + 1, NC * c, NC * c + 1]
 
@@ -98,15 +102,22 @@
         copy.start()
 
     barrier = pltpu.get_barrier_semaphore()
-    greeted = [device(x, (z + step) % NZ, y, c) for step in Z_STEPS if min(step, NZ - step) <= NZ // 4]
-    greeted += [at(offset(x, y, dx, dy), (c + dc) % NC) for dx, dy, dc in PLANE_CORE_STEPS]
+    greeted = [device(x, mod(z + step, NZ), y, c) for step in Z_STEPS if min(step, NZ - step) <= NZ // 4]
+    greeted += [at(offset(x, y, dx, dy), mod(c + dc, NC)) for dx, dy, dc in PLANE_CORE_STEPS]
     for other in greeted:
         pl.semaphore_signal(barrier, inc=1, device_id={"dp": other}, device_id_type=pl.DeviceIdType.MESH)
 
     loads[0].wait()
     start_hi, start_lo = split2(start[...].T)
 
+    def core_copy(h):
+        return remote(give.at[h], core_in.at[h], core_s.at[h], core_r.at[h], sibling)
+
     for i in range(PARTS):
+        if i == NC:
+            pl.semaphore_wait(barrier, len(greeted))
+            for h in range(HALVES):
+                core_copy(h).start()
         loads[1 + i].wait()
         hi, lo = split2(emb[i])
         emb_hi[i] = hi
@@ -115,19 +126,13 @@
         store, j = (give, i) if i < NC else (part, i - NC)
         store[:, :, :, j * WIDE:(j + 1) * WIDE] = total.reshape(HALVES, PLANE, 8, WIDE)
 
-    pl.semaphore_wait(barrier, len(greeted))
     for step in (NZ // 4, NZ - NZ // 4):
-        pl.semaphore_signal(relay, inc=1, device_id={"dp": device(x, (z + step) % NZ, y, c)}, device_id_type=pl.DeviceIdType.MESH)
-
-    def core_copy(h):
-        return remote(give.at[h], core_in.at[h], core_s.at[h], core_r.at[h], sibling)
+        pl.semaphore_signal(relay, inc=1, device_id={"dp": device(x, mod(z + step, NZ), y, c)}, device_id_type=pl.DeviceIdType.MESH)
 
     def plane_copy(h, o):
         q = offset(x, y, *PLANE_STEPS[o])
         return remote(part.at[h, q], plane_in.at[h, o], xs.at[h], xr.at[h], at(q, c))
 
-    for h in range(HALVES):
-        core_copy(h).start()
     for h in range(HALVES):
         core_copy(h).wait_recv()
         part[h] = part[h] + core_in[h]
@@ -140,7 +145,7 @@
         return 4 * t + NC * h + c
 
     def z_copy(h, t):
-        step = (keeper(h, t) - z + NZ) % NZ
+        step = mod(keeper(h, t) - z + NZ, NZ)
         return remote(tiles.at[h, t], z_in.at[step], zs.at[h, t], zr.at[0], device(x, keeper(h, t), y, c))
 
     for h in range(HALVES):
@@ -161,13 +166,13 @@
     def tile_of(h, t):
         return sketch.at[h, p, :, lanes(c * OWN + t * 128, 128)]
 
-    mine = z // 4
+    mine = lax.div(z, 4)
 
     def z_out(h, step):
-        return remote(tile_of(h, mine), tile_of(h, mine), ags.at[0], agr.at[h, mine], device(x, (z + step) % NZ, y, c))
+        return remote(tile_of(h, mine), tile_of(h, mine), ags.at[0], agr.at[h, mine], device(x, mod(z + step, NZ), y, c))
 
     def keeps(h):
-        return z % 4 == NC * h + c
+        return mod(z, 4) == NC * h + c
 
     for h in range(HALVES):
         @pl.when(keeps(h))
@@ -224,17 +229,17 @@
             forward(h, o).start()
         halves.append(image_part(h, c))
 
-    keeps_a = y % NC == c
+    keeps_a = mod(y, NC) == c
 
     pairs = [(s, dc) for s in range(PLANE) for dc in range(NC) if (s, dc) != (0, 0)]
 
     def gram_a(s):
         q = offset(x, y, *around[s])
-        slot = NC * s + ((q % NY) + c) % NC
-        return remote(gram_part.at[0, q], gram_in_a.at[slot], gas.at[s], gar.at[0], at(q, (q % NY) % NC))
+        slot = NC * s + mod(q + c, NC)
+        return remote(gram_part.at[0, q], gram_in_a.at[slot], gas.at[s], gar.at[0], at(q, mod(q, NC)))
 
     def gram_b(s, dc):
-        q, core = offset(x, y, *around[s]), (c + dc) % NC
+        q, core = offset(x, y, *around[s]), mod(c + dc, NC)
         return remote(gram_part.at[1 + core, q], gram_in_b.at[NC * s + dc], gbs.at[0], gbr.at[0], at(q, core))
 
     pieces = []
@@ -259,7 +264,7 @@
                 gram_b(s, dc).start()
 
     def gram_z_copy(store, send, recv, step):
-        return remote(store.at[z], store.at[z], send.at[0], recv.at[0], device(x, (z + step) % NZ, y, c))
+        return remote(store.at[z], store.at[z], send.at[0], recv.at[0], device(x, mod(z + step, NZ), y, c))
 
     @pl.when(keeps_a)
     def _():
@@ -280,7 +285,7 @@
         gram_z_copy(gram_z_b, hbs, hbr, step).start()
 
     image[...] = jnp.concatenate(halves, 0).T
-    image_copy = pltpu.make_async_copy(image, image_hbm, out_sem)
+    image_copy = pltpu.make_async_copy(image, image_hbm, out_sem.at[0])
     image_copy.start()
     for h in range(HALVES):
         core_copy(h).wait_send()
@@ -312,32 +317,36 @@
         return total
 
     def gram_out_a(s, dc):
-        block = gram_all.at[0, p]
-        return remote(block, block, kas.at[0], kar.at[0], at(offset(x, y, *around[s]), (c + dc) % NC))
+        block = gram_a_all.at[p]
+        return remote(block, block, kas.at[0], kar.at[0], at(offset(x, y, *around[s]), mod(c + dc, NC)))
 
     def gram_out_b(s, dc):
-        block = gram_all.at[1 + c, p]
-        return remote(block, block, kbs.at[0], kbr.at[0], at(offset(x, y, *around[s]), (c + dc) % NC))
+        other = at(offset(x, y, *around[s]), mod(c + dc, NC))
+        return remote(gram_b_own, gram_hbm.at[c, p], kbs.at[0], kbr.at[0], other)
 
     @pl.when(keeps_a)
     def _():
-        gram_all[0, p] = z_sum(gram_z_a, har)
+        gram_a_all[p] = z_sum(gram_z_a, har)
         for s, dc in pairs:
             gram_out_a(s, dc).start()
 
-    gram_all[1 + c, p] = z_sum(gram_z_b, hbr)
+    gram_b_own[...] = z_sum(gram_z_b, hbr)
     for s, dc in pairs:
         gram_out_b(s, dc).start()
+    own_copy = pltpu.make_async_copy(gram_b_own, gram_hbm.at[c, p], out_sem.at[1])
+    own_copy.start()
 
     @pl.when(keeps_a)
     def _():
-        landed(gram_all.at[0, pl.ds(0, PLANE - 1)], kar.at[0])
+        landed(gram_a_all.at[pl.ds(0, PLANE - 1)], kar.at[0])
 
     @pl.when(jnp.logical_not(keeps_a))
     def _():
-        landed(gram_all.at[0], kar.at[0])
-
-    first_ref[...] = first_inverse(gram_all[0].reshape(HALF, HALF))
+        landed(gram_a_all, kar.at[0])
+
+    first[...] = first_inverse(gram_a_all[...].reshape(HALF, HALF))
+    first_copy = pltpu.make_async_copy(first, first_hbm, out_sem.at[2])
+    first_copy.start()
 
     @pl.when(keeps_a)
     def _():
@@ -347,9 +356,10 @@
     landed(gram_z_b.at[pl.ds(0, NZ - 1)], hbs.at[0])
     landed(gram_in_b.at[pl.ds(1, 31)], kbs.at[0])
     image_copy.wait()
+    own_copy.wait()
+    first_copy.wait()
 
     landed(gram_in_b.at[pl.ds(1, 31)], kbr.at[0])
-    gram_ref[...] = gram_all[1:3].reshape(NC, HALF, HALF)
 
 
 def sums(embeddings, start_basis):
@@ -360,11 +370,11 @@
         gather_kernel,
         out_shape=(
             jax.ShapeDtypeStruct((rows, K), F32),
-            jax.ShapeDtypeStruct((NC, HALF, HALF), F32),
+            jax.ShapeDtypeStruct((NC, PLANE, 8, 128), F32),
             jax.ShapeDtypeStruct((HALF, HALF), F32),
         ),
         in_specs=[pl.BlockSpec(memory_space=pl.ANY)] * 2,
-        out_specs=(pl.BlockSpec(memory_space=pl.ANY),) + (pl.BlockSpec(memory_space=pltpu.VMEM),) * 2,
+        out_specs=(pl.BlockSpec(memory_space=pl.ANY),) * 3,
         scratch_shapes=[
             vmem((PARTS, rows, WIDE), F32),
             vmem((PARTS, rows, WIDE), BF16),
@@ -383,7 +393,9 @@
             vmem((32, 8, 128), F32),
             vmem((NZ, 8, 128), F32),
             vmem((NZ, 8, 128), F32),
-            vmem((3, PLANE, 8, 128), F32),
+            vmem((PLANE, 8, 128), F32),
+            vmem((8, 128), F32),
+            vmem((HALF, HALF), F32),
             dma(PARTS + 1),
             dma(HALVES), dma(HALVES),
             dma(HALVES), dma(HALVES),
@@ -397,7 +409,7 @@
             dma(1), dma(1),
             dma(1), dma(1),
             dma(1), dma(1),
-            pltpu.SemaphoreType.DMA,
+            dma(3),
             pltpu.SemaphoreType.REGULAR,
         ],
         compiler_params=pltpu.CompilerParams(
@@ -498,16 +510,22 @@
     return inverse * row
 
 
-def basis_kernel(scale, gram_ref, first_ref, image_hbm, out_hbm, image, out, sems):
-    copy = pltpu.make_async_copy(image_hbm, image, sems.at[0])
-    copy.start()
-    first = first_ref[...]
-    ba, bb = gram_ref[0], gram_ref[1]
+def basis_kernel(scale, gram_hbm, first_hbm, image_hbm, out_hbm, gram, first_in, image, out, sems):
+    loads = [
+        pltpu.make_async_copy(src, dst, sems.at[i])
+        for i, (src, dst) in enumerate([(gram_hbm, gram), (first_hbm, first_in), (image_hbm, image)])
+    ]
+    for copy in loads:
+        copy.start()
+    loads[0].wait()
+    ba, bb = gram[0].reshape(HALF, HALF), gram[1].reshape(HALF, HALF)
     col, row = diagonal_scales(bb)
+    loads[1].wait()
+    first = first_in[...]
     cross = mm6(ba * col, first, NT)
     rest = bb * col * row - mm6(cross, cross, NT)
     lower = mm6(cross, first, NN)
-    copy.wait()
+    loads[2].wait()
     rows = image.shape[0]
     outs = []
 
@@ -518,7 +536,7 @@
         return both[:, :HALF] + (both[:, HALF:] + mm(lo, high, NT))
 
     def leave(r, n, cols):
-        outs.append(pltpu.make_async_copy(out.at[pl.ds(r, n), cols], out_hbm.at[pl.ds(r, n), cols], sems.at[1 + len(outs)]))
+        outs.append(pltpu.make_async_copy(out.at[pl.ds(r, n), cols], out_hbm.at[pl.ds(r, n), cols], sems.at[3 + len(outs)]))
         outs[-1].start()
 
     out[:, :HALF] = product(image[:, :HALF], first * scale)
@@ -535,13 +553,18 @@
 
 def basis_of(gram, first, image, scale):
     rows = image.shape[0]
-    in_vmem = pl.BlockSpec(memory_space=pltpu.VMEM)
     return pl.pallas_call(
         functools.partial(basis_kernel, scale),
         out_shape=jax.ShapeDtypeStruct((rows, K), F32),
-        in_specs=[in_vmem, in_vmem, pl.BlockSpec(memory_space=pl.ANY)],
+        in_specs=[pl.BlockSpec(memory_space=pl.ANY)] * 3,
         out_specs=pl.BlockSpec(memory_space=pl.ANY),
-        scratch_shapes=[pltpu.VMEM((rows, K), F32), pltpu.VMEM((rows, K), F32), pltpu.SemaphoreType.DMA((4,))],
+        scratch_shapes=[
+            pltpu.VMEM((NC, PLANE, 8, 128), F32),
+            pltpu.VMEM((HALF, HALF), F32),
+            pltpu.VMEM((rows, K), F32),
+            pltpu.VMEM((rows, K), F32),
+            pltpu.SemaphoreType.DMA((6,)),
+        ],
         compiler_params=pltpu.CompilerParams(vmem_limit_bytes=VMEM_BYTES),
         name="basis",
     )(gram, first, image)

time: 75.1 us -> 73.9 us (0.984)
  Pallas kernels: 74.7 us -> 73.6 us
where the time goes in v5:
time: 73.9 us; the launch traced here: 73.8 us
  Pallas kernels  73.6 us (100%)
    pallas_call x1, Pallas kernels, sums(): pl.pallas_call(gather_kernel, out_shape=(jax.ShapeDtypeStruct((rows, K),...  67.9 us
    pallas_call x1, Pallas kernels, basis_of(): pl.pallas_call(functools.partial(basis_kernel, scale), out_shape=jax.Shap...  5.7 us

profile of v5, /device:TPU:1, one launch (start us, length us, event | category | flops | bytes accessed | tf_op | source)
XLA Modules:
  0.0 73.8 jit_solution(15204546894564484762)
XLA Ops:
  0.0 67.9 %sums.1 = (f32[832,256]{1,0:T(8,128)}, f32[2,16,8,128]{3,2,1,0:T(8,128)}, f32[128,128]{1,0:T(8,128)}) custom-call(f32[832,1024]{1,0:T(8,128)} %emb_hbm.1, f32[832,256]{1,0:T(8,128)} %start_hbm.1), custom_call_target="tpu_custom_call" | custom-call | tf_op jit(solution)/shard_map/sums/pallas_call | solution.py:369
  67.9 5.7 %basis.1 = f32[832,256]{1,0:T(8,128)} custom-call(f32[2,16,8,128]{3,2,1,0:T(8,128)} %get-tuple-element.8.gram_hbm, f32[128,128]{1,0:T(8,128)} %get-tuple-element.9.first_hbm, f32[832,256]{1,0:T(8,128)} %get-tuple-element.10.image_hbm), custom_call_target="tpu_custom_call" | custom-call | tf_op jit(solution)/shard_map/basis/pallas_call | solution.py:556

commit v6 on v5

--- a/solution.py
+++ b/solution.py
@@ -227,7 +227,8 @@
             block = block_of(h, source(o), c)
             landed(block, br.at[h, o])
             forward(h, o).start()
-        halves.append(image_part(h, c))
+        if h == 0:
+            halves.append(image_part(h, c))
 
     keeps_a = mod(y, NC) == c
 
@@ -244,6 +245,8 @@
 
     pieces = []
     for h in range(HALVES):
+        if h == 1:
+            halves.append(image_part(h, c))
         landed(part.at[h], fr.at[h])
         halves[h] = halves[h] + image_part(h, 1 - c)
         pieces += split2(halves[h])
@@ -487,9 +490,9 @@
 
 
 def mm6(a, b, dims):
-    ah, am, al = split3(a)
-    bh, bm, bl = split3(b)
-    return mm(ah, bh, dims) + (mm(ah, bm, dims) + mm(am, bh, dims)) + (mm(am, bm, dims) + (mm(ah, bl, dims) + mm(al, bh, dims)))
+    ((left,), (right,)), _ = dims
+    pa, pb = split3(a), split3(b)
+    return mm(jnp.concatenate([pa[i] for i in LEFT], left), jnp.concatenate([pb[i] for i in RIGHT], right), dims)
 
 
 def diagonal():

time: 73.9 us -> 73.2 us (level)
  no operation moved by 1% of the time
where the time goes in v6:
time: 73.2 us; the launch traced here: 73.1 us
  Pallas kernels  72.9 us (100%)
    pallas_call x1, Pallas kernels, sums(): pl.pallas_call(gather_kernel, out_shape=(jax.ShapeDtypeStruct((rows, K),...  67.4 us
    pallas_call x1, Pallas kernels, basis_of(): pl.pallas_call(functools.partial(basis_kernel, scale), out_shape=jax.Shap...  5.57 us

profile of v6, /device:TPU:1, one launch (start us, length us, event | category | flops | bytes accessed | tf_op | source)
XLA Modules:
  0.0 73.1 jit_solution(1687859173186173974)
XLA Ops:
  0.0 67.4 %sums.1 = (f32[832,256]{1,0:T(8,128)}, f32[2,16,8,128]{3,2,1,0:T(8,128)}, f32[128,128]{1,0:T(8,128)}) custom-call(f32[832,1024]{1,0:T(8,128)} %emb_hbm.1, f32[832,256]{1,0:T(8,128)} %start_hbm.1), custom_call_target="tpu_custom_call" | custom-call | tf_op jit(solution)/shard_map/sums/pallas_call | solution.py:372
  67.4 5.6 %basis.1 = f32[832,256]{1,0:T(8,128)} custom-call(f32[2,16,8,128]{3,2,1,0:T(8,128)} %get-tuple-element.8.gram_hbm, f32[128,128]{1,0:T(8,128)} %get-tuple-element.9.first_hbm, f32[832,256]{1,0:T(8,128)} %get-tuple-element.10.image_hbm), custom_call_target="tpu_custom_call" | custom-call | tf_op jit(solution)/shard_map/basis/pallas_call | solution.py:559

commit v7 on v6

--- a/solution.py
+++ b/solution.py
@@ -222,13 +222,14 @@
         return total
 
     halves = []
-    for h in range(HALVES):
+    def pass_on(h):
         for o in reversed(range(PLANE - 1)):
             block = block_of(h, source(o), c)
             landed(block, br.at[h, o])
             forward(h, o).start()
-        if h == 0:
-            halves.append(image_part(h, c))
+
+    pass_on(0)
+    halves.append(image_part(0, c))
 
     keeps_a = mod(y, NC) == c
 
@@ -246,6 +247,7 @@
     pieces = []
     for h in range(HALVES):
         if h == 1:
+            pass_on(h)
             halves.append(image_part(h, c))
         landed(part.at[h], fr.at[h])
         halves[h] = halves[h] + image_part(h, 1 - c)

time: 73.2 us -> 72.4 us (0.989)
  Pallas kernels: 72.9 us -> 72.1 us
    pallas_call x1, Pallas kernels: 67.4 us -> 66.6 us  [sums(): pl.pallas_call(gather_kernel, out_shape=(jax.ShapeDtypeStruct((rows, K),...]
where the time goes in v7:
time: 72.4 us; the launch traced here: 72.3 us
  Pallas kernels  72.1 us (100%)
    pallas_call x1, Pallas kernels, sums(): pl.pallas_call(gather_kernel, out_shape=(jax.ShapeDtypeStruct((rows, K),...  66.6 us
    pallas_call x1, Pallas kernels, basis_of(): pl.pallas_call(functools.partial(basis_kernel, scale), out_shape=jax.Shap...  5.56 us

profile of v7, /device:TPU:1, one launch (start us, length us, event | category | flops | bytes accessed | tf_op | source)
XLA Modules:
  0.0 72.3 jit_solution(5412714358814059408)
XLA Ops:
  0.0 66.6 %sums.1 = (f32[832,256]{1,0:T(8,128)}, f32[2,16,8,128]{3,2,1,0:T(8,128)}, f32[128,128]{1,0:T(8,128)}) custom-call(f32[832,1024]{1,0:T(8,128)} %emb_hbm.1, f32[832,256]{1,0:T(8,128)} %start_hbm.1), custom_call_target="tpu_custom_call" | custom-call | tf_op jit(solution)/shard_map/sums/pallas_call | solution.py:374
  66.6 5.6 %basis.1 = f32[832,256]{1,0:T(8,128)} custom-call(f32[2,16,8,128]{3,2,1,0:T(8,128)} %get-tuple-element.8.gram_hbm, f32[128,128]{1,0:T(8,128)} %get-tuple-element.9.first_hbm, f32[832,256]{1,0:T(8,128)} %get-tuple-element.10.image_hbm), custom_call_target="tpu_custom_call" | custom-call | tf_op jit(solution)/shard_map/basis/pallas_call | solution.py:561

commit v8 on v7

--- a/solution.py
+++ b/solution.py
@@ -233,7 +233,7 @@
 
     keeps_a = mod(y, NC) == c
 
-    pairs = [(s, dc) for s in range(PLANE) for dc in range(NC) if (s, dc) != (0, 0)]
+    pairs = [(s, dc) for s in range(1, PLANE) for dc in range(NC)] + [(0, 1)]
 
     def gram_a(s):
         q = offset(x, y, *around[s])
@@ -548,7 +548,7 @@
     leave(0, rows, pl.ds(0, HALF))
     below, second = eliminate([rest, -lower, jnp.where(diagonal(), 1.0, 0.0)])
     factor = jnp.concatenate([below, second * row], 1) * scale
-    step = rows // 2
+    step = rows // 4
     for r in range(0, rows, step):
         out[r:r + step, HALF:] = product(image[r:r + step, :], factor)
         leave(r, step, pl.ds(HALF, HALF))
@@ -568,7 +568,7 @@
             pltpu.VMEM((HALF, HALF), F32),
             pltpu.VMEM((rows, K), F32),
             pltpu.VMEM((rows, K), F32),
-            pltpu.SemaphoreType.DMA((6,)),
+            pltpu.SemaphoreType.DMA((8,)),
         ],
         compiler_params=pltpu.CompilerParams(vmem_limit_bytes=VMEM_BYTES),
         name="basis",

time: 72.4 us -> 72.4 us (level)
  no operation moved by 1% of the time
where the time goes in v8:
time: 72.4 us; the launch traced here: 72.3 us
  Pallas kernels  72.1 us (100%)
    pallas_call x1, Pallas kernels, sums(): pl.pallas_call(gather_kernel, out_shape=(jax.ShapeDtypeStruct((rows, K),...  66.6 us
    pallas_call x1, Pallas kernels, basis_of(): pl.pallas_call(functools.partial(basis_kernel, scale), out_shape=jax.Shap...  5.55 us

profile of v8, /device:TPU:1, one launch (start us, length us, event | category | flops | bytes accessed | tf_op | source)
XLA Modules:
  0.0 72.3 jit_solution(2802634703127617406)
XLA Ops:
  0.0 66.6 %sums.1 = (f32[832,256]{1,0:T(8,128)}, f32[2,16,8,128]{3,2,1,0:T(8,128)}, f32[128,128]{1,0:T(8,128)}) custom-call(f32[832,1024]{1,0:T(8,128)} %emb_hbm.1, f32[832,256]{1,0:T(8,128)} %start_hbm.1), custom_call_target="tpu_custom_call" | custom-call | tf_op jit(solution)/shard_map/sums/pallas_call | solution.py:374
  66.6 5.5 %basis.1 = f32[832,256]{1,0:T(8,128)} custom-call(f32[2,16,8,128]{3,2,1,0:T(8,128)} %get-tuple-element.8.gram_hbm, f32[128,128]{1,0:T(8,128)} %get-tuple-element.9.first_hbm, f32[832,256]{1,0:T(8,128)} %get-tuple-element.10.image_hbm), custom_call_target="tpu_custom_call" | custom-call | tf_op jit(solution)/shard_map/basis/pallas_call | solution.py:561
